TPU v7x, 512 devices: a whole 4x8x8 slice. The times are simulated.
512 devices in a mesh: ctx: 32 (over y_lo, z, core), ch: 16 (over y_hi, x).
Axes of the slice: x: 4, y: 8 (y_hi: 4, y_lo: 2; y = y_hi * 2 + y_lo), z: 8, core: 2. Of those that a mesh axis runs over, the one named last changes fastest.
Arguments:
- query_proj: bfloat16 [4096, 4096], P('ctx', 'ch'), may hold values from -6 to 6
- key_proj: bfloat16 [4096, 4096], P('ctx', 'ch'), may hold values from -6 to 6
- value_proj: bfloat16 [4096, 4096], P('ctx', 'ch'), may hold values from -6 to 6
- cotangent: bfloat16 [4096, 4096], P('ctx', 'ch'), may hold values from -6 to 6
- filter_basis: bfloat16 [4096, 64], P('ctx'), may hold values from -6 to 6
- filter_weight: bfloat16 [64, 4096], P(None, 'ch'), may hold values from -0.125 to 0.125
- decay_rate: float32 [4096], P('ch'), may hold values from 6.1035156e-05 to 0.0014648438
- skip_weight: float32 [4096], P('ch'), may hold values from 0.5 to 1.5
- norm_gain: float32 [4096], P('ch'), may hold values from 0.1 to 1.9
Outputs:
- output: bfloat16 [4096, 4096], P('ctx', 'ch')
- grad_query: bfloat16 [4096, 4096], P('ctx', 'ch')
- grad_key: bfloat16 [4096, 4096], P('ctx', 'ch')
- grad_value: bfloat16 [4096, 4096], P('ctx', 'ch')
- grad_filter: float32 [64, 4096], P('ctx', 'ch')
All inputs are finite; a program needn't handle non-finite values.
Results may differ from a plain program's by a relative error of at most 0.0015.
Values sent between devices are 32-bit elements; how exact they have to be, the bound alone decides.
A program may use at most 64 MiB of HBM per device.

v0:
```python
import math

import jax
import jax.numpy as jnp
from jax import lax
from jax.sharding import PartitionSpec as P

exact_precision = lax.Precision.HIGHEST


def from_partner(block, axis, distance):
    count = lax.axis_size(axis)
    route = []
    for low in range(count):
        high = low | 1 << distance
        if high != low and high < count:
            route += [(low, high), (high, low)]
    return lax.ppermute(block, axis, route)


def dft_table(points, sign):
    index_row = jnp.arange(points, dtype=jnp.int32)
    product = index_row[:, None] * index_row[None, :] % points
    angles = sign * 2.0 * math.pi * product.astype(jnp.float32) / points
    return (jnp.cos(angles), jnp.sin(angles))


def complex_rows(cos_table, sin_table, current, form, out_axis):
    real_part = current[:, 0]
    imag_part = current[:, 1]
    points = cos_table.shape[0]
    stacked = jnp.concatenate([cos_table, sin_table], 0)
    from_real = jnp.einsum(form, stacked, real_part, precision=exact_precision)
    from_imag = jnp.einsum(form, stacked, imag_part, precision=exact_precision)
    real_cos = lax.slice_in_dim(from_real, 0, points, axis=out_axis)
    real_sin = lax.slice_in_dim(from_real, points, 2 * points, axis=out_axis)
    imag_cos = lax.slice_in_dim(from_imag, 0, points, axis=out_axis)
    imag_sin = lax.slice_in_dim(from_imag, points, 2 * points, axis=out_axis)
    return jnp.stack([real_cos - imag_sin, imag_cos + real_sin], 1)


def complex_scale(current, cos_w, sin_w):
    real_part = current[:, 0]
    imag_part = current[:, 1]
    return jnp.stack(
        [real_part * cos_w - imag_part * sin_w, real_part * sin_w + imag_part * cos_w], 1
    )


def complex_mul(left, right, flip):
    left_real = left[:, 0]
    left_imag = -left[:, 1] if flip else left[:, 1]
    right_real = right[:, 0]
    right_imag = right[:, 1]
    return jnp.stack(
        [
            left_real * right_real - left_imag * right_imag,
            left_real * right_imag + left_imag * right_real,
        ],
        1,
    )


def twist(signal, angles):
    cos_w = jnp.cos(angles)
    sin_w = jnp.sin(angles)
    real_part = jnp.stack([signal, signal * cos_w], 1)
    imag_part = jnp.stack([jnp.zeros_like(signal), signal * sin_w], 1)
    return jnp.stack([real_part, imag_part], 1)


def untwist(current, angles):
    even_part = current[:, 0, 0]
    odd_real = current[:, 0, 1]
    odd_imag = current[:, 1, 1]
    return 0.5 * (even_part + jnp.cos(angles) * odd_real - jnp.sin(angles) * odd_imag)


def section_turn(ctx_rank, block_rows, half_span):
    local_index = ctx_rank * block_rows % half_span + jnp.arange(block_rows, dtype=jnp.int32)
    angles = -math.pi * local_index.astype(jnp.float32) / half_span
    return (jnp.cos(angles)[:, None], jnp.sin(angles)[:, None])


def spread_butterfly(signals):
    block_rows = signals.shape[1]
    ctx_count = lax.axis_size("ctx")
    levels = ctx_count.bit_length() - 1
    ctx_rank = lax.axis_index("ctx")
    full_length = block_rows * ctx_count
    position = (ctx_rank * block_rows + jnp.arange(block_rows, dtype=jnp.int32)).astype(jnp.float32)
    current = twist(signals, (-math.pi * position / full_length)[:, None])
    for level_index in range(levels):
        swap_bit = levels - 1 - level_index
        half_span = full_length >> level_index + 1
        is_upper = ctx_rank >> swap_bit & 1 == 1
        cos_w, sin_w = section_turn(ctx_rank, block_rows, half_span)
        sign_own = jnp.where(is_upper, -1.0, 1.0)
        cos_pick = jnp.where(is_upper, cos_w, 1.0)
        sin_pick = jnp.where(is_upper, sin_w, 0.0)
        partner = from_partner(current, "ctx", swap_bit)
        current = complex_scale(partner + sign_own * current, cos_pick, sin_pick)
    cos_table, sin_table = dft_table(block_rows, -1.0)
    return complex_rows(cos_table, sin_table, current, "kj,shjc->shkc", 2)


def gather_butterfly(spectra):
    block_rows = spectra.shape[3]
    ctx_count = lax.axis_size("ctx")
    levels = ctx_count.bit_length() - 1
    ctx_rank = lax.axis_index("ctx")
    full_length = block_rows * ctx_count
    cos_table, sin_table = dft_table(block_rows, 1.0)
    current = complex_rows(cos_table, sin_table, spectra, "kj,shjc->shkc", 2) / block_rows
    for level_index in reversed(range(levels)):
        swap_bit = levels - 1 - level_index
        half_span = full_length >> level_index + 1
        is_upper = ctx_rank >> swap_bit & 1 == 1
        cos_w, sin_w = section_turn(ctx_rank, block_rows, half_span)
        own_cos = jnp.where(is_upper, -cos_w, 1.0)
        own_sin = jnp.where(is_upper, sin_w, 0.0)
        other_cos = jnp.where(is_upper, 1.0, cos_w)
        other_sin = jnp.where(is_upper, 0.0, -sin_w)
        partner = from_partner(current, "ctx", swap_bit)
        current = 0.5 * (
            complex_scale(current, own_cos, own_sin) + complex_scale(partner, other_cos, other_sin)
        )
    position = (ctx_rank * block_rows + jnp.arange(block_rows, dtype=jnp.int32)).astype(jnp.float32)
    return untwist(current, (math.pi * position / full_length)[:, None])


def shards(
    query_proj,
    key_proj,
    value_proj,
    cotangent,
    filter_basis,
    filter_weight,
    decay_rate,
    skip_weight,
    norm_gain,
):
    block_rows, width = query_proj.shape
    ctx_rank = lax.axis_index("ctx")
    full_width = width * lax.axis_size("ch")
    position = (ctx_rank * block_rows + jnp.arange(block_rows, dtype=jnp.int32)).astype(jnp.float32)
    decay = jnp.exp(-decay_rate[None, :] * position[:, None])
    kernel = jnp.dot(filter_basis, filter_weight, preferred_element_type=jnp.float32) * decay
    queries = query_proj.astype(jnp.float32)
    keys_full = key_proj.astype(jnp.float32)
    values_full = value_proj.astype(jnp.float32)
    gated = keys_full * values_full
    spectra = spread_butterfly(jnp.stack([gated, kernel], 0))
    conv = gather_butterfly(complex_mul(spectra[0:1], spectra[1:2], False))[0]
    mixed = conv + skip_weight[None, :] * gated
    signal = queries * mixed
    scaled = norm_gain[None, :] * cotangent.astype(jnp.float32)
    square_sum = lax.psum(jnp.sum(signal * signal, axis=1), "ch")
    inv_rms = lax.rsqrt(square_sum / full_width + 1e-06)
    output = (signal * inv_rms[:, None] * norm_gain[None, :]).astype(jnp.bfloat16)
    slope = lax.psum(jnp.sum(signal * scaled, axis=1), "ch")
    grad_signal = inv_rms[:, None] * scaled - signal * (inv_rms**3 * slope / full_width)[:, None]
    grad_query = (grad_signal * mixed).astype(jnp.bfloat16)
    grad_mixed = grad_signal * queries
    grad_spec = spread_butterfly(grad_mixed[None])
    both_terms = gather_butterfly(
        complex_mul(jnp.concatenate([spectra[1:2], spectra[0:1]], 0), grad_spec, True)
    )
    grad_gated = both_terms[0] + skip_weight[None, :] * grad_mixed
    grad_key = (grad_gated * values_full).astype(jnp.bfloat16)
    grad_value = (grad_gated * keys_full).astype(jnp.bfloat16)
    grad_kernel = both_terms[1] * decay
    basis_part = filter_basis.astype(jnp.float32)
    grad_filter = lax.psum_scatter(
        jnp.dot(basis_part.T, grad_kernel, precision=exact_precision),
        "ctx",
        scatter_dimension=0,
        tiled=True,
    )
    return (output, grad_query, grad_key, grad_value, grad_filter)


def solution(mesh):
    return jax.shard_map(
        shards,
        mesh=mesh,
        in_specs=(
            P("ctx", "ch"),
            P("ctx", "ch"),
            P("ctx", "ch"),
            P("ctx", "ch"),
            P("ctx", None),
            P(None, "ch"),
            P("ch"),
            P("ch"),
            P("ch"),
        ),
        out_specs=(P("ctx", "ch"), P("ctx", "ch"), P("ctx", "ch"), P("ctx", "ch"), P("ctx", "ch")),
        check_vma=False,
    )
```

profile of v0, /device:TPU:1, one launch (start us, length us, event | category | flops | bytes accessed | tf_op | source)
XLA Modules:
  0.0 752.5 jit_solution(8524345872979995694)
XLA Ops:
  7.3 0.7 copy-done.37
  8.0 0.9 fusion.93
  9.5 4.0 collective-permute-start
  13.6 17.9 %collective-permute-done = f32[2,2,2,128,256]{4,3,2,0,1:T(8,128)S(1)} collective-permute-done((f32[2,2,2,128,256]{4,3,2,0,1:T(8,128)S(1)}, f32[2,2,2,128,256]{4,3,2,0,1:T(8,128)S(1)}, u32[]{:S(2)}, u32[]{:S(2)}) %collective-permute-start) | collective-permute-done | bytes 1048608 | tf_op jit(solution)/shard_map/ppermute | solution.py:18
  31.9 15.4 %collective-permute-start.1 = (f32[2,2,2,128,256]{4,3,2,0,1:T(8,128)S(1)}, f32[2,2,2,128,256]{4,3,2,0,1:T(8,128)S(1)}, u32[]{:S(2)}, u32[]{:S(2)}) collective-permute-start(f32[2,2,2,128,256]{4,3,2,0,1:T(8,128)S(1)} %pad_maximum_fusion.2), channel_id=1, source_target_pairs={{0,128},{128,0},{16,144},{144,16},{32,160},{160,32},{48,176},{176,... | collective-permute-start | bytes 3145736 | tf_op jit(solution)/shard_map/ppermute | solution.py:18
  47.4 22.0 %collective-permute-done.1 = f32[2,2,2,128,256]{4,3,2,0,1:T(8,128)S(1)} collective-permute-done((f32[2,2,2,128,256]{4,3,2,0,1:T(8,128)S(1)}, f32[2,2,2,128,256]{4,3,2,0,1:T(8,128)S(1)}, u32[]{:S(2)}, u32[]{:S(2)}) %collective-permute-start.1) | collective-permute-done | bytes 1048608 | tf_op jit(solution)/shard_map/ppermute | solution.py:18
  69.8 28.0 %collective-permute-start.2 = (f32[2,2,2,128,256]{4,3,2,0,1:T(8,128)S(1)}, f32[2,2,2,128,256]{4,3,2,0,1:T(8,128)S(1)}, u32[]{:S(2)}, u32[]{:S(2)}) collective-permute-start(f32[2,2,2,128,256]{4,3,2,0,1:T(8,128)S(1)} %pad_maximum_fusion.3), channel_id=1, source_target_pairs={{0,64},{64,0},{16,80},{80,16},{32,96},{96,32},{48,112},{112,48},{1... | collective-permute-start | bytes 3145736 | tf_op jit(solution)/shard_map/ppermute | solution.py:18
  97.9 45.7 %collective-permute-done.2 = f32[2,2,2,128,256]{4,3,2,0,1:T(8,128)S(1)} collective-permute-done((f32[2,2,2,128,256]{4,3,2,0,1:T(8,128)S(1)}, f32[2,2,2,128,256]{4,3,2,0,1:T(8,128)S(1)}, u32[]{:S(2)}, u32[]{:S(2)}) %collective-permute-start.2) | collective-permute-done | bytes 1048608 | tf_op jit(solution)/shard_map/ppermute | solution.py:18
  144.0 1.9 collective-permute-start.3
  146.0 24.1 %collective-permute-done.3 = f32[2,2,2,128,256]{4,3,2,0,1:T(8,128)S(1)} collective-permute-done((f32[2,2,2,128,256]{4,3,2,0,1:T(8,128)S(1)}, f32[2,2,2,128,256]{4,3,2,0,1:T(8,128)S(1)}, u32[]{:S(2)}, u32[]{:S(2)}) %collective-permute-start.3) | collective-permute-done | bytes 1048608 | tf_op jit(solution)/shard_map/ppermute | solution.py:18
  170.6 3.2 collective-permute-start.4
  174.5 1.6 collective-permute-done.4
  176.3 1.1 convolution_bitcast_fusion.2
  177.4 1.1 convolution_bitcast_fusion.3
  178.6 0.6 convolution_bitcast_fusion.6
  179.2 0.6 convolution_bitcast_fusion.7
  180.0 2.3 collective-permute-start.5
  182.5 1.3 collective-permute-done.5
  184.0 1.9 collective-permute-start.6
  186.0 0.6 copy-done.18
  186.8 12.3 %collective-permute-done.6 = f32[1,2,2,128,256]{4,3,2,1,0:T(8,128)S(1)} collective-permute-done((f32[1,2,2,128,256]{4,3,2,1,0:T(8,128)S(1)}, f32[1,2,2,128,256]{4,3,2,1,0:T(8,128)S(1)}, u32[]{:S(2)}, u32[]{:S(2)}) %collective-permute-start.6) | collective-permute-done | bytes 524320 | tf_op jit(solution)/shard_map/ppermute | solution.py:18
  199.2 1.9 collective-permute-start.7
  201.3 0.6 copy-done.16
  202.0 24.8 %collective-permute-done.7 = f32[1,2,2,128,256]{4,3,2,1,0:T(8,128)S(1)} collective-permute-done((f32[1,2,2,128,256]{4,3,2,1,0:T(8,128)S(1)}, f32[1,2,2,128,256]{4,3,2,1,0:T(8,128)S(1)}, u32[]{:S(2)}, u32[]{:S(2)}) %collective-permute-start.7) | collective-permute-done | bytes 524320 | tf_op jit(solution)/shard_map/ppermute | solution.py:18
  227.1 6.9 collective-permute-start.8
  234.1 0.6 copy-done.14
  234.8 22.4 %collective-permute-done.8 = f32[1,2,2,128,256]{4,3,2,1,0:T(8,128)S(1)} collective-permute-done((f32[1,2,2,128,256]{4,3,2,1,0:T(8,128)S(1)}, f32[1,2,2,128,256]{4,3,2,1,0:T(8,128)S(1)}, u32[]{:S(2)}, u32[]{:S(2)}) %collective-permute-start.8) | collective-permute-done | bytes 524320 | tf_op jit(solution)/shard_map/ppermute | solution.py:18
  257.4 3.2 collective-permute-start.9
  260.8 0.6 copy-done.12
  261.5 9.8 %collective-permute-done.9 = f32[1,2,2,128,256]{4,3,2,1,0:T(8,128)S(1)} collective-permute-done((f32[1,2,2,128,256]{4,3,2,1,0:T(8,128)S(1)}, f32[1,2,2,128,256]{4,3,2,1,0:T(8,128)S(1)}, u32[]{:S(2)}, u32[]{:S(2)}) %collective-permute-start.9) | collective-permute-done | bytes 524320 | tf_op jit(solution)/shard_map/ppermute | solution.py:18
  271.6 0.7 copy-done.2
  272.6 38.2 %all-reduce.3 = (f32[128]{0:T(128)S(1)}, f32[128]{0:T(128)S(1)}) all-reduce(f32[128]{0:T(128)S(1)} %get-tuple-element.6, f32[128]{0:T(128)S(1)} %get-tuple-element.5), channel_id=1, replica_groups=mesh['ctx'=32,'ch'=16] {'ch'}, use_global_device_ids=true, to_apply=%region_1.2 | all-reduce | flops 256 | bytes 2048 | tf_op jit(solution)/shard_map/psum | solution.py:158
  310.9 0.7 copy-done.36
  311.5 0.8 multiply_bitcast_fusion.1
  312.3 0.7 copy-done.34
  313.1 2.4 collective-permute-start.10
  315.5 7.6 %collective-permute-done.10 = f32[1,2,2,128,256]{4,3,2,1,0:T(8,128)S(1)} collective-permute-done((f32[1,2,2,128,256]{4,3,2,1,0:T(8,128)S(1)}, f32[1,2,2,128,256]{4,3,2,1,0:T(8,128)S(1)}, u32[]{:S(2)}, u32[]{:S(2)}) %collective-permute-start.10) | collective-permute-done | bytes 524320 | tf_op jit(solution)/shard_map/ppermute | solution.py:18
  323.3 4.4 collective-permute-start.11
  327.8 11.9 %collective-permute-done.11 = f32[1,2,2,128,256]{4,3,2,1,0:T(8,128)S(1)} collective-permute-done((f32[1,2,2,128,256]{4,3,2,1,0:T(8,128)S(1)}, f32[1,2,2,128,256]{4,3,2,1,0:T(8,128)S(1)}, u32[]{:S(2)}, u32[]{:S(2)}) %collective-permute-start.11) | collective-permute-done | bytes 524320 | tf_op jit(solution)/shard_map/ppermute | solution.py:18
  340.0 1.9 collective-permute-start.12
  341.9 14.3 %collective-permute-done.12 = f32[1,2,2,128,256]{4,3,2,1,0:T(8,128)S(1)} collective-permute-done((f32[1,2,2,128,256]{4,3,2,1,0:T(8,128)S(1)}, f32[1,2,2,128,256]{4,3,2,1,0:T(8,128)S(1)}, u32[]{:S(2)}, u32[]{:S(2)}) %collective-permute-start.12) | collective-permute-done | bytes 524320 | tf_op jit(solution)/shard_map/ppermute | solution.py:18
  356.4 5.8 collective-permute-start.13
  362.2 12.2 %collective-permute-done.13 = f32[1,2,2,128,256]{4,3,2,1,0:T(8,128)S(1)} collective-permute-done((f32[1,2,2,128,256]{4,3,2,1,0:T(8,128)S(1)}, f32[1,2,2,128,256]{4,3,2,1,0:T(8,128)S(1)}, u32[]{:S(2)}, u32[]{:S(2)}) %collective-permute-start.13) | collective-permute-done | bytes 524320 | tf_op jit(solution)/shard_map/ppermute | solution.py:18
  374.7 12.3 %collective-permute-start.14 = (f32[1,2,2,128,256]{4,3,2,1,0:T(8,128)S(1)}, f32[1,2,2,128,256]{4,3,2,1,0:T(8,128)S(1)}, u32[]{:S(2)}, u32[]{:S(2)}) collective-permute-start(f32[1,2,2,128,256]{4,3,2,1,0:T(8,128)S(1)} %pad_maximum_fusion.10), channel_id=1, source_target_pairs={{0,16},{16,0},{32,48},{48,32},{64,80},{80,64},{96,112},{112,96},{1... | collective-permute-start | bytes 1572872 | tf_op jit(solution)/shard_map/ppermute | solution.py:18
  387.1 1.2 collective-permute-done.14
  388.4 0.7 convolution_bitcast_fusion.4
  389.1 0.7 convolution_bitcast_fusion.5
  389.8 1.1 convolution_bitcast_fusion
  390.9 1.1 convolution_bitcast_fusion.1
  392.2 2.3 collective-permute-start.15
  394.7 2.1 collective-permute-done.15
  397.1 1.9 collective-permute-start.16
  399.3 24.1 %collective-permute-done.16 = f32[2,2,2,128,256]{4,3,2,0,1:T(8,128)S(1)} collective-permute-done((f32[2,2,2,128,256]{4,3,2,0,1:T(8,128)S(1)}, f32[2,2,2,128,256]{4,3,2,0,1:T(8,128)S(1)}, u32[]{:S(2)}, u32[]{:S(2)}) %collective-permute-start.16) | collective-permute-done | bytes 1048608 | tf_op jit(solution)/shard_map/ppermute | solution.py:18
  423.8 5.0 collective-permute-start.17
  429.0 45.8 %collective-permute-done.17 = f32[2,2,2,128,256]{4,3,2,0,1:T(8,128)S(1)} collective-permute-done((f32[2,2,2,128,256]{4,3,2,0,1:T(8,128)S(1)}, f32[2,2,2,128,256]{4,3,2,0,1:T(8,128)S(1)}, u32[]{:S(2)}, u32[]{:S(2)}) %collective-permute-start.17) | collective-permute-done | bytes 1048608 | tf_op jit(solution)/shard_map/ppermute | solution.py:18
  475.2 2.6 collective-permute-start.18
  478.0 48.0 %collective-permute-done.18 = f32[2,2,2,128,256]{4,3,2,0,1:T(8,128)S(1)} collective-permute-done((f32[2,2,2,128,256]{4,3,2,0,1:T(8,128)S(1)}, f32[2,2,2,128,256]{4,3,2,0,1:T(8,128)S(1)}, u32[]{:S(2)}, u32[]{:S(2)}) %collective-permute-start.18) | collective-permute-done | bytes 1048608 | tf_op jit(solution)/shard_map/ppermute | solution.py:18
  526.4 2.5 collective-permute-start.19
  528.9 1.3 dynamic-slice
  531.1 21.0 %collective-permute-done.19 = f32[2,2,2,128,256]{4,3,2,0,1:T(8,128)S(1)} collective-permute-done((f32[2,2,2,128,256]{4,3,2,0,1:T(8,128)S(1)}, f32[2,2,2,128,256]{4,3,2,0,1:T(8,128)S(1)}, u32[]{:S(2)}, u32[]{:S(2)}) %collective-permute-start.19) | collective-permute-done | bytes 1048608 | tf_op jit(solution)/shard_map/ppermute | solution.py:18
  553.1 0.9 convolution_bitcast_fusion.8
  554.0 0.7 fusion.69
  554.7 189.7 %all-reduce.6.cloned.1.call-done = f32[64,256]{1,0:T(8,128)} async-done(((f32[64,256]{1,0:T(8,128)}), f32[64,256]{1,0:T(8,128)}) %all-reduce.6.cloned.1.call-update) | async-done | bytes 65552
  744.4 1.3 constant_dynamic-slice_fusion
  (168 shorter events, 10.8 us)
Async XLA Ops:
  7.2 1.8 copy-start
  7.2 737.2 %all-reduce.6.cloned.1.call-start = ((), (), s32[]{:S(2)}) async-start(), calls=%async_computation | async-start | bytes 131072
  7.3 1.9 copy-start.33
  7.3 2.0 copy-start.35
  7.3 0.7 copy-start.37
  8.0 0.9 copy-start.31
  8.0 0.9 copy-start.19
  8.0 0.9 copy-start.6
  9.5 22.0 %collective-permute-start = (f32[2,2,2,128,256]{4,3,2,0,1:T(8,128)S(1)}, f32[2,2,2,128,256]{4,3,2,0,1:T(8,128)S(1)}, u32[]{:S(2)}, u32[]{:S(2)}) collective-permute-start(f32[2,2,2,128,256]{4,3,2,0,1:T(8,128)S(1)} %pad_maximum_fusion.1), channel_id=1, source_target_pairs={{0,256},{256,0},{16,272},{272,16},{32,288},{288,32},{48,304},{304,... | collective-permute-start | bytes 3145736 | tf_op jit(solution)/shard_map/ppermute | solution.py:18
  13.6 18.0 %copy-start.11 = (f32[128]{0:T(128)}, f32[128]{0:T(128)S(1)}, u32[]{:S(2)}) copy-start(f32[128]{0:T(128)S(1)} %get-tuple-element.90) | copy-start | bytes 1540
  13.6 18.0 %copy-start.21 = (f32[128]{0:T(128)}, f32[128]{0:T(128)S(1)}, u32[]{:S(2)}) copy-start(f32[128]{0:T(128)S(1)} %get-tuple-element.91) | copy-start | bytes 1540
  31.9 37.5 %collective-permute-start.1 = (f32[2,2,2,128,256]{4,3,2,0,1:T(8,128)S(1)}, f32[2,2,2,128,256]{4,3,2,0,1:T(8,128)S(1)}, u32[]{:S(2)}, u32[]{:S(2)}) collective-permute-start(f32[2,2,2,128,256]{4,3,2,0,1:T(8,128)S(1)} %pad_maximum_fusion.2), channel_id=1, source_target_pairs={{0,128},{128,0},{16,144},{144,16},{32,160},{160,32},{48,176},{176,... | collective-permute-start | bytes 3145736 | tf_op jit(solution)/shard_map/ppermute | solution.py:18
  47.4 22.2 %copy-start.13 = (f32[128]{0:T(128)}, f32[128]{0:T(128)S(1)}, u32[]{:S(2)}) copy-start(f32[128]{0:T(128)S(1)} %get-tuple-element.94) | copy-start | bytes 1540
  47.4 22.2 %copy-start.23 = (f32[128]{0:T(128)}, f32[128]{0:T(128)S(1)}, u32[]{:S(2)}) copy-start(f32[128]{0:T(128)S(1)} %get-tuple-element.95) | copy-start | bytes 1540
  69.8 73.8 %collective-permute-start.2 = (f32[2,2,2,128,256]{4,3,2,0,1:T(8,128)S(1)}, f32[2,2,2,128,256]{4,3,2,0,1:T(8,128)S(1)}, u32[]{:S(2)}, u32[]{:S(2)}) collective-permute-start(f32[2,2,2,128,256]{4,3,2,0,1:T(8,128)S(1)} %pad_maximum_fusion.3), channel_id=1, source_target_pairs={{0,64},{64,0},{16,80},{80,16},{32,96},{96,32},{48,112},{112,48},{1... | collective-permute-start | bytes 3145736 | tf_op jit(solution)/shard_map/ppermute | solution.py:18
  97.9 45.8 %copy-start.15 = (f32[128]{0:T(128)}, f32[128]{0:T(128)S(1)}, u32[]{:S(2)}) copy-start(f32[128]{0:T(128)S(1)} %get-tuple-element.98) | copy-start | bytes 1540
  97.9 45.8 %copy-start.25 = (f32[128]{0:T(128)}, f32[128]{0:T(128)S(1)}, u32[]{:S(2)}) copy-start(f32[128]{0:T(128)S(1)} %get-tuple-element.99) | copy-start | bytes 1540
  144.0 26.2 %collective-permute-start.3 = (f32[2,2,2,128,256]{4,3,2,0,1:T(8,128)S(1)}, f32[2,2,2,128,256]{4,3,2,0,1:T(8,128)S(1)}, u32[]{:S(2)}, u32[]{:S(2)}) collective-permute-start(f32[2,2,2,128,256]{4,3,2,0,1:T(8,128)S(1)} %pad_maximum_fusion.4), channel_id=1, source_target_pairs={{0,32},{32,0},{16,48},{48,16},{64,96},{96,64},{80,112},{112,80},{1... | collective-permute-start | bytes 3145736 | tf_op jit(solution)/shard_map/ppermute | solution.py:18
  146.0 24.3 %copy-start.17 = (f32[128]{0:T(128)}, f32[128]{0:T(128)S(1)}, u32[]{:S(2)}) copy-start(f32[128]{0:T(128)S(1)} %get-tuple-element.102) | copy-start | bytes 1540
  146.0 24.3 %copy-start.27 = (f32[128]{0:T(128)}, f32[128]{0:T(128)S(1)}, u32[]{:S(2)}) copy-start(f32[128]{0:T(128)S(1)} %get-tuple-element.103) | copy-start | bytes 1540
  170.6 5.5 collective-permute-start.4
  173.9 3.4 copy-start.9
  173.9 8.4 %copy-start.7 = (f32[128]{0:T(128)}, f32[128]{0:T(128)S(1)}, u32[]{:S(2)}) copy-start(f32[128]{0:T(128)S(1)} %get-tuple-element.106) | copy-start | bytes 1540
  180.0 3.8 collective-permute-start.5
  184.0 15.0 %collective-permute-start.6 = (f32[1,2,2,128,256]{4,3,2,1,0:T(8,128)S(1)}, f32[1,2,2,128,256]{4,3,2,1,0:T(8,128)S(1)}, u32[]{:S(2)}, u32[]{:S(2)}) collective-permute-start(f32[1,2,2,128,256]{4,3,2,1,0:T(8,128)S(1)} %fusion.10), channel_id=1, source_target_pairs={{0,32},{32,0},{16,48},{48,16},{64,96},{96,64},{80,112},{112,80},{1... | collective-permute-start | bytes 1572872 | tf_op jit(solution)/shard_map/ppermute | solution.py:18
  186.0 0.7 copy-start.18
  199.2 27.6 %collective-permute-start.7 = (f32[1,2,2,128,256]{4,3,2,1,0:T(8,128)S(1)}, f32[1,2,2,128,256]{4,3,2,1,0:T(8,128)S(1)}, u32[]{:S(2)}, u32[]{:S(2)}) collective-permute-start(f32[1,2,2,128,256]{4,3,2,1,0:T(8,128)S(1)} %fusion.11), channel_id=1, source_target_pairs={{0,64},{64,0},{16,80},{80,16},{32,96},{96,32},{48,112},{112,48},{1... | collective-permute-start | bytes 1572872 | tf_op jit(solution)/shard_map/ppermute | solution.py:18
  201.2 0.7 copy-start.16
  227.1 30.1 %collective-permute-start.8 = (f32[1,2,2,128,256]{4,3,2,1,0:T(8,128)S(1)}, f32[1,2,2,128,256]{4,3,2,1,0:T(8,128)S(1)}, u32[]{:S(2)}, u32[]{:S(2)}) collective-permute-start(f32[1,2,2,128,256]{4,3,2,1,0:T(8,128)S(1)} %fusion.12), channel_id=1, source_target_pairs={{0,128},{128,0},{16,144},{144,16},{32,160},{160,32},{48,176},{176,... | collective-permute-start | bytes 1572872 | tf_op jit(solution)/shard_map/ppermute | solution.py:18
  234.0 0.7 copy-start.14
  257.4 13.9 %collective-permute-start.9 = (f32[1,2,2,128,256]{4,3,2,1,0:T(8,128)S(1)}, f32[1,2,2,128,256]{4,3,2,1,0:T(8,128)S(1)}, u32[]{:S(2)}, u32[]{:S(2)}) collective-permute-start(f32[1,2,2,128,256]{4,3,2,1,0:T(8,128)S(1)} %fusion.13), channel_id=1, source_target_pairs={{0,256},{256,0},{16,272},{272,16},{32,288},{288,32},{48,304},{304,... | collective-permute-start | bytes 1572872 | tf_op jit(solution)/shard_map/ppermute | solution.py:18
  260.7 0.6 copy-start.12
  271.5 0.8 copy-start.2
  271.5 0.9 copy-start.3
  271.5 0.9 copy-start.4
  271.5 0.9 copy-start.5
  271.5 0.9 copy-start.30
  271.6 0.8 copy-start.29
  310.9 0.7 copy-start.36
  312.3 0.7 copy-start.34
  313.1 10.0 %copy-start.22 = (f32[128]{0:T(128)S(1)}, f32[128]{0:T(128)}, u32[]{:S(2)}) copy-start(f32[128]{0:T(128)} %copy-done.21) | copy-start | bytes 1540
  313.1 9.9 %collective-permute-start.10 = (f32[1,2,2,128,256]{4,3,2,1,0:T(8,128)S(1)}, f32[1,2,2,128,256]{4,3,2,1,0:T(8,128)S(1)}, u32[]{:S(2)}, u32[]{:S(2)}) collective-permute-start(f32[1,2,2,128,256]{4,3,2,1,0:T(8,128)S(1)} %pad_maximum_fusion.6), channel_id=1, source_target_pairs={{0,256},{256,0},{16,272},{272,16},{32,288},{288,32},{48,304},{304,... | collective-permute-start | bytes 1572872 | tf_op jit(solution)/shard_map/ppermute | solution.py:18
  323.3 16.4 %copy-start.24 = (f32[128]{0:T(128)S(1)}, f32[128]{0:T(128)}, u32[]{:S(2)}) copy-start(f32[128]{0:T(128)} %copy-done.23) | copy-start | bytes 1540
  323.3 16.3 %collective-permute-start.11 = (f32[1,2,2,128,256]{4,3,2,1,0:T(8,128)S(1)}, f32[1,2,2,128,256]{4,3,2,1,0:T(8,128)S(1)}, u32[]{:S(2)}, u32[]{:S(2)}) collective-permute-start(f32[1,2,2,128,256]{4,3,2,1,0:T(8,128)S(1)} %pad_maximum_fusion.7), channel_id=1, source_target_pairs={{0,128},{128,0},{16,144},{144,16},{32,160},{160,32},{48,176},{176,... | collective-permute-start | bytes 1572872 | tf_op jit(solution)/shard_map/ppermute | solution.py:18
  340.0 16.3 %copy-start.26 = (f32[128]{0:T(128)S(1)}, f32[128]{0:T(128)}, u32[]{:S(2)}) copy-start(f32[128]{0:T(128)} %copy-done.25) | copy-start | bytes 1540
  340.0 16.2 %collective-permute-start.12 = (f32[1,2,2,128,256]{4,3,2,1,0:T(8,128)S(1)}, f32[1,2,2,128,256]{4,3,2,1,0:T(8,128)S(1)}, u32[]{:S(2)}, u32[]{:S(2)}) collective-permute-start(f32[1,2,2,128,256]{4,3,2,1,0:T(8,128)S(1)} %pad_maximum_fusion.8), channel_id=1, source_target_pairs={{0,64},{64,0},{16,80},{80,16},{32,96},{96,32},{48,112},{112,48},{1... | collective-permute-start | bytes 1572872 | tf_op jit(solution)/shard_map/ppermute | solution.py:18
  356.4 18.1 %copy-start.28 = (f32[128]{0:T(128)S(1)}, f32[128]{0:T(128)}, u32[]{:S(2)}) copy-start(f32[128]{0:T(128)} %copy-done.27) | copy-start | bytes 1540
  356.4 18.0 %collective-permute-start.13 = (f32[1,2,2,128,256]{4,3,2,1,0:T(8,128)S(1)}, f32[1,2,2,128,256]{4,3,2,1,0:T(8,128)S(1)}, u32[]{:S(2)}, u32[]{:S(2)}) collective-permute-start(f32[1,2,2,128,256]{4,3,2,1,0:T(8,128)S(1)} %pad_maximum_fusion.9), channel_id=1, source_target_pairs={{0,32},{32,0},{16,48},{48,16},{64,96},{96,64},{80,112},{112,80},{1... | collective-permute-start | bytes 1572872 | tf_op jit(solution)/shard_map/ppermute | solution.py:18
  374.7 13.6 %collective-permute-start.14 = (f32[1,2,2,128,256]{4,3,2,1,0:T(8,128)S(1)}, f32[1,2,2,128,256]{4,3,2,1,0:T(8,128)S(1)}, u32[]{:S(2)}, u32[]{:S(2)}) collective-permute-start(f32[1,2,2,128,256]{4,3,2,1,0:T(8,128)S(1)} %pad_maximum_fusion.10), channel_id=1, source_target_pairs={{0,16},{16,0},{32,48},{48,32},{64,80},{80,64},{96,112},{112,96},{1... | collective-permute-start | bytes 1572872 | tf_op jit(solution)/shard_map/ppermute | solution.py:18
  387.1 1.3 copy-start.8
  387.1 1.3 copy-start.10
  392.2 4.6 collective-permute-start.15
  397.1 26.3 %collective-permute-start.16 = (f32[2,2,2,128,256]{4,3,2,0,1:T(8,128)S(1)}, f32[2,2,2,128,256]{4,3,2,0,1:T(8,128)S(1)}, u32[]{:S(2)}, u32[]{:S(2)}) collective-permute-start(f32[2,2,2,128,256]{4,3,2,0,1:T(8,128)S(1)} %fusion.1), channel_id=1, source_target_pairs={{0,32},{32,0},{16,48},{48,16},{64,96},{96,64},{80,112},{112,80},{1... | collective-permute-start | bytes 3145736 | tf_op jit(solution)/shard_map/ppermute | solution.py:18
  423.8 51.0 %collective-permute-start.17 = (f32[2,2,2,128,256]{4,3,2,0,1:T(8,128)S(1)}, f32[2,2,2,128,256]{4,3,2,0,1:T(8,128)S(1)}, u32[]{:S(2)}, u32[]{:S(2)}) collective-permute-start(f32[2,2,2,128,256]{4,3,2,0,1:T(8,128)S(1)} %fusion.2), channel_id=1, source_target_pairs={{0,64},{64,0},{16,80},{80,16},{32,96},{96,32},{48,112},{112,48},{1... | collective-permute-start | bytes 3145736 | tf_op jit(solution)/shard_map/ppermute | solution.py:18
  475.2 50.9 %collective-permute-start.18 = (f32[2,2,2,128,256]{4,3,2,0,1:T(8,128)S(1)}, f32[2,2,2,128,256]{4,3,2,0,1:T(8,128)S(1)}, u32[]{:S(2)}, u32[]{:S(2)}) collective-permute-start(f32[2,2,2,128,256]{4,3,2,0,1:T(8,128)S(1)} %fusion.3), channel_id=1, source_target_pairs={{0,128},{128,0},{16,144},{144,16},{32,160},{160,32},{48,176},{176,... | collective-permute-start | bytes 3145736 | tf_op jit(solution)/shard_map/ppermute | solution.py:18
  526.4 25.7 %collective-permute-start.19 = (f32[2,2,2,128,256]{4,3,2,0,1:T(8,128)S(1)}, f32[2,2,2,128,256]{4,3,2,0,1:T(8,128)S(1)}, u32[]{:S(2)}, u32[]{:S(2)}) collective-permute-start(f32[2,2,2,128,256]{4,3,2,0,1:T(8,128)S(1)} %fusion.4), channel_id=1, source_target_pairs={{0,256},{256,0},{16,272},{272,16},{32,288},{288,32},{48,304},{304,... | collective-permute-start | bytes 3145736 | tf_op jit(solution)/shard_map/ppermute | solution.py:18
  552.4 0.7 copy-start.20
  552.4 0.7 copy-start.32
  554.0 191.7 %copy-start.1 = (bf16[64,256]{1,0:T(8,128)(2,1)S(1)}, bf16[64,256]{1,0:T(8,128)(2,1)}, u32[]{:S(2)}) copy-start(bf16[64,256]{1,0:T(8,128)(2,1)} %param.14) | copy-start | bytes 98308
Sparse Core Ops, SparseCore 0:
  554.1 190.2 all-reduce.5
where the time goes:
time: 754 us; the launch traced here: 753 us
  waiting for transfers between devices  560 us (74%)
  starting transfers between devices  110 us (15%)
  blocking collectives  38.2 us (5%)
  between operations  16 us (2%)
  other arithmetic  12.1 us (2%)
  local copies, waits for them, and re-layouts  8.47 us (1%)
  matrix products  8.03 us (1%)
    ppermute x20, waiting for transfers between devices, from_partner(): return lax.ppermute(block, axis, route)  370 us
    unnamed x2, waiting for transfers between devices  190 us
    ppermute x20, starting transfers between devices, from_partner(): return lax.ppermute(block, axis, route)  110 us
    psum x1, blocking collectives, shards(): square_sum = lax.psum(jnp.sum(signal * signal, axis=1), 'ch')  38.2 us
  transfers between devices with their start and end apart: 21, of which 21 were waited for; matrix products, arithmetic and copies ran while one was open for 1% of the time, Pallas kernels for 0%

commit v1 on v0

v1 whole, which is shorter than its diff:
```python
import functools
import math

import jax
import jax.numpy as jnp
import ml_dtypes
import numpy as np
from jax import lax
from jax.experimental import pallas as pl
from jax.experimental.pallas import tpu as pltpu
from jax.sharding import PartitionSpec as P

MESH = pl.DeviceIdType.MESH
F32 = jnp.float32
BF16 = jnp.bfloat16


def halves(table):
    high = table.astype(np.float32).astype(ml_dtypes.bfloat16)
    low = (table - high.astype(np.float64)).astype(ml_dtypes.bfloat16)
    return high, low


def transform_tables(blocks, rows, group):
    half = 2 * blocks
    odd = 2 * np.arange(blocks) + 1
    angle = math.pi * odd[:, None] * np.arange(blocks)[None, :] / half
    eye = np.eye(group)
    cos_part = np.kron(np.cos(angle), eye)
    sin_part = np.kron(np.sin(angle), eye)
    outer = np.concatenate([cos_part, -sin_part], 0)
    outer_back = np.concatenate([cos_part.T, -sin_part.T], 1) / (blocks * rows)
    index = np.arange(rows)
    inner_angle = 2.0 * math.pi * (index[:, None] * index[None, :] % rows) / rows
    inner_cos, inner_sin = np.cos(inner_angle), -np.sin(inner_angle)
    inner = np.block([[inner_cos, inner_sin], [-inner_sin, inner_cos]])
    turn = np.repeat(math.pi * odd[:, None] * index[None, :] / (half * rows), group, 0)
    turns = np.stack([np.cos(turn), -np.sin(turn)]).astype(np.float32)
    return (*halves(outer), *halves(outer_back), *halves(inner), turns)


def split(x):
    high = x.astype(BF16)
    return high, (x - high.astype(F32)).astype(BF16)


def dot(a, b):
    return jnp.dot(a, b, preferred_element_type=F32)


def dot3(a, b):
    return dot(a[0], b[0]) + dot(a[0], b[1]) + dot(a[1], b[0])


def kernel(
    n_ctx, n_ch,
    q_ref, k_ref, v_ref, ct_ref, basis_ref, weight_ref, rate_ref, skip_ref, gain_ref,
    outer_hi, outer_lo, back_hi, back_lo, inner_hi, inner_lo, turns,
    out_ref, gq_ref, gk_ref, gv_ref, gf_ref,
    send_g, send_k, send_c, send_m, send_x, send_y, send_s, send_f,
    recv_g, recv_k, recv_c, recv_m, recv_x, recv_y, recv_s, recv_f,
    send_sem, recv_sem,
):
    rows, width = q_ref.shape
    group = width // n_ctx
    full_width = width * n_ch
    me = lax.axis_index("ctx")
    my_ch = lax.axis_index("ch")

    barrier = pltpu.get_barrier_semaphore()

    def greet_ctx(d, carry):
        to = lax.rem(me + d, n_ctx)
        pl.semaphore_signal(barrier, inc=1, device_id={"ctx": to}, device_id_type=MESH)
        return carry

    def greet_ch(d, carry):
        to = lax.rem(my_ch + d, n_ch)
        pl.semaphore_signal(barrier, inc=1, device_id={"ch": to}, device_id_type=MESH)
        return carry

    lax.fori_loop(1, n_ctx, greet_ctx, 0)
    lax.fori_loop(1, n_ch, greet_ch, 0)

    def exchange(slot, src, dst):
        def step(d, carry):
            to = lax.rem(me + d, n_ctx)
            pltpu.make_async_remote_copy(
                src_ref=src.at[pl.ds(pl.multiple_of(to * group, group), group)],
                dst_ref=dst.at[pl.ds(pl.multiple_of(me * group, group), group)],
                send_sem=send_sem.at[slot],
                recv_sem=recv_sem.at[slot],
                device_id={"ctx": to},
                device_id_type=MESH,
            ).start()
            return carry

        lax.fori_loop(1, n_ctx, step, 0)
        own = pl.ds(pl.multiple_of(me * group, group), group)
        dst[own] = src[own]

    def all_of(slot, src, dst, extent, axis, count):
        return pltpu.make_async_remote_copy(
            src_ref=src.at[extent],
            dst_ref=dst.at[extent],
            send_sem=send_sem.at[slot],
            recv_sem=recv_sem.at[slot],
            device_id={axis: count},
            device_id_type=MESH,
        )

    others = pl.ds(0, (n_ctx - 1) * group)
    neighbour = lax.rem(me + 1, n_ctx)

    def arrived(slot, src, dst):
        all_of(slot, src, dst, others, "ctx", neighbour).wait_recv()

    def left(slot, src, dst):
        all_of(slot, src, dst, others, "ctx", neighbour).wait_send()

    outer = (outer_hi[...], outer_lo[...])
    back = (back_hi[...], back_lo[...])
    inner = (inner_hi[...], inner_lo[...])
    turn_cos, turn_sin = turns[0], turns[1]

    def turned(real, imag):
        return jnp.concatenate(
            [real * turn_cos - imag * turn_sin, real * turn_sin + imag * turn_cos], 1
        )

    def forward(blocks):
        first = dot3(outer, split(jnp.concatenate(blocks, 1)))
        parts = []
        for at in range(len(blocks)):
            columns = slice(at * rows, (at + 1) * rows)
            parts.append(turned(first[:width, columns], first[width:, columns]))
        spectra = dot3(split(jnp.concatenate(parts, 0)), inner)
        return [
            (spectra[at * width : (at + 1) * width, :rows], spectra[at * width : (at + 1) * width, rows:])
            for at in range(len(blocks))
        ]

    def inverse(conjugates):
        stacked = jnp.concatenate([jnp.concatenate(pair, 1) for pair in conjugates], 0)
        first = dot3(split(stacked), inner)
        columns = []
        for at in range(len(conjugates)):
            part = first[at * width : (at + 1) * width]
            z = turned(part[:, :rows], part[:, rows:])
            columns.append(jnp.concatenate([z[:, :rows], -z[:, rows:]], 0))
        return dot3(back, split(jnp.concatenate(columns, 1)))

    position = (me * rows + lax.broadcasted_iota(jnp.int32, (rows, width), 0)).astype(F32)
    decay = jnp.exp(-rate_ref[...] * position)
    filter_block = dot(basis_ref[...], weight_ref[...]) * decay
    send_k[...] = filter_block.T
    keys = k_ref[...].astype(F32)
    values = v_ref[...].astype(F32)
    gated = (keys * values).T
    send_g[...] = gated

    pl.semaphore_wait(barrier, n_ctx + n_ch - 2)
    exchange(0, send_k, recv_k)
    exchange(1, send_g, recv_g)

    queries = q_ref[...].astype(F32).T
    scaled = (ct_ref[...].astype(F32) * gain_ref[...]).T
    skip = jnp.broadcast_to(skip_ref[...], (rows, width)).T
    gain = gain_ref[...]

    arrived(0, send_k, recv_k)
    arrived(1, send_g, recv_g)
    gated_spec, kernel_spec = forward([recv_g[...], recv_k[...]])

    def product(a, b):
        return a[0] * b[0] - a[1] * b[1], a[0] * b[1] + a[1] * b[0]

    def conj(a):
        return a[0], -a[1]

    send_c[...] = inverse([conj(product(gated_spec, kernel_spec))])
    exchange(2, send_c, recv_c)
    arrived(2, send_c, recv_c)

    mixed = recv_c[...] + skip * gated
    signal = queries * mixed
    send_s[0:1] = jnp.sum(signal * signal, axis=0, keepdims=True)
    send_s[1:2] = jnp.sum(signal * scaled, axis=0, keepdims=True)

    def share(d, carry):
        to = lax.rem(my_ch + d, n_ch)
        pltpu.make_async_remote_copy(
            src_ref=send_s,
            dst_ref=recv_s.at[my_ch],
            send_sem=send_sem.at[3],
            recv_sem=recv_sem.at[3],
            device_id={"ch": to},
            device_id_type=MESH,
        ).start()
        return carry

    lax.fori_loop(1, n_ch, share, 0)
    recv_s[my_ch] = send_s[...]
    sums_wait = pltpu.make_async_remote_copy(
        src_ref=recv_s.at[pl.ds(0, n_ch - 1)],
        dst_ref=recv_s.at[pl.ds(0, n_ch - 1)],
        send_sem=send_sem.at[3],
        recv_sem=recv_sem.at[3],
        device_id={"ch": lax.rem(my_ch + 1, n_ch)},
        device_id_type=MESH,
    )
    sums_wait.wait_recv()
    sums = jnp.sum(recv_s[...], axis=0)
    inv_rms = lax.rsqrt(sums[0:1] / full_width + 1e-06)
    pull = inv_rms * inv_rms * inv_rms * sums[1:2] / full_width
    grad_signal = inv_rms * scaled - signal * pull
    grad_mixed = grad_signal * queries
    send_m[...] = grad_mixed
    exchange(4, send_m, recv_m)

    out_ref[...] = ((signal * inv_rms).T * gain).astype(BF16)
    gq_ref[...] = (grad_signal * mixed).T.astype(BF16)

    arrived(4, send_m, recv_m)
    (grad_spec,) = forward([recv_m[...]])
    both = inverse(
        [product(gated_spec, conj(grad_spec)), product(kernel_spec, conj(grad_spec))]
    )
    send_x[...] = both[:, :rows]
    exchange(5, send_x, recv_x)
    send_y[...] = both[:, rows:]
    exchange(6, send_y, recv_y)

    arrived(5, send_x, recv_x)
    grad_kernel = split(recv_x[...].T * decay)
    basis = basis_ref[...].astype(F32).T.astype(BF16)
    share_f = dot(basis, grad_kernel[0]) + dot(basis, grad_kernel[1])
    each = share_f.shape[0] // n_ctx
    for at in range(n_ctx):
        send_f[at] = share_f[at * each : (at + 1) * each]

    def scatter(d, carry):
        to = lax.rem(me + d, n_ctx)
        pltpu.make_async_remote_copy(
            src_ref=send_f.at[to],
            dst_ref=recv_f.at[me],
            send_sem=send_sem.at[7],
            recv_sem=recv_sem.at[7],
            device_id={"ctx": to},
            device_id_type=MESH,
        ).start()
        return carry

    lax.fori_loop(1, n_ctx, scatter, 0)
    recv_f[me] = send_f[me]

    arrived(6, send_y, recv_y)
    grad_gated = (recv_y[...] + skip * grad_mixed).T
    gk_ref[...] = (grad_gated * values).astype(BF16)
    gv_ref[...] = (grad_gated * keys).astype(BF16)

    filter_wait = all_of(7, send_f, recv_f, pl.ds(0, n_ctx - 1), "ctx", neighbour)
    filter_wait.wait_recv()
    gf_ref[...] = jnp.sum(recv_f[...], axis=0)

    left(0, send_k, recv_k)
    left(1, send_g, recv_g)
    left(2, send_c, recv_c)
    sums_wait.wait_send()
    left(4, send_m, recv_m)
    left(5, send_x, recv_x)
    left(6, send_y, recv_y)
    filter_wait.wait_send()


def solution(mesh):
    n_ctx, n_ch = mesh.shape["ctx"], mesh.shape["ch"]

    def shards(query, key, value, cotangent, basis, weight, rate, skip, gain):
        rows, width = query.shape
        features = basis.shape[1]
        each = features // n_ctx
        tables = transform_tables(n_ctx, rows, width // n_ctx)
        whole = pl.BlockSpec(memory_space=pltpu.VMEM)
        block = (width, rows)
        wide = jax.ShapeDtypeStruct((rows, width), BF16)
        slots = [pltpu.VMEM(block, F32)] * 6
        return pl.pallas_call(
            functools.partial(kernel, n_ctx, n_ch),
            out_shape=(wide, wide, wide, wide, jax.ShapeDtypeStruct((each, width), F32)),
            in_specs=[whole] * (9 + len(tables)),
            out_specs=(whole,) * 5,
            scratch_shapes=[
                *slots,
                pltpu.VMEM((2, rows), F32),
                pltpu.VMEM((n_ctx, each, width), F32),
                *slots,
                pltpu.VMEM((n_ch, 2, rows), F32),
                pltpu.VMEM((n_ctx, each, width), F32),
                pltpu.SemaphoreType.DMA((8,)),
                pltpu.SemaphoreType.DMA((8,)),
            ],
            compiler_params=pltpu.CompilerParams(
                collective_id=0, has_side_effects=True, vmem_limit_bytes=48 * 1024 * 1024
            ),
        )(
            query, key, value, cotangent, basis, weight,
            rate[None, :], skip[None, :], gain[None, :],
            *(jnp.asarray(table) for table in tables),
        )

    return jax.shard_map(
        shards,
        mesh=mesh,
        in_specs=(
            P("ctx", "ch"), P("ctx", "ch"), P("ctx", "ch"), P("ctx", "ch"),
            P("ctx", None), P(None, "ch"), P("ch"), P("ch"), P("ch"),
        ),
        out_specs=(P("ctx", "ch"),) * 5,
        check_vma=False,
    )
```

time: 754 us -> 75.6 us (0.10)
  waiting for transfers between devices: 560 us -> 0 us
  starting transfers between devices: 110 us -> 0 us
  Pallas kernels: 0 us -> 60.5 us
  blocking collectives: 38.2 us -> 0 us
  between operations: 16 us -> 0.73 us
  other arithmetic: 12.1 us -> 0 us
  matrix products: 8.03 us -> 0 us
    ppermute x20 -> x0, waiting for transfers between devices: 370 us -> none  [from_partner(): return lax.ppermute(block, axis, route)]
    unnamed x2 -> x0, waiting for transfers between devices: 190 us -> none
    ppermute x20 -> x0, starting transfers between devices: 110 us -> none  [from_partner(): return lax.ppermute(block, axis, route)]
    pallas_call x0 -> x1, Pallas kernels: none -> 60.5 us  [shards(): pl.pallas_call(functools.partial(kernel, n_ctx, n_ch), out_shape=(wide, w...]
    psum x1 -> x0, blocking collectives: 38.2 us -> none  [shards(): square_sum = lax.psum(jnp.sum(signal * signal, axis=1), 'ch')]
    dot_general x10 -> x0, matrix products: 8.03 us -> none  [the longest x4 3.47 us: complex_rows(): from_imag = jnp.einsum(form, stacked, imag_part, precision=exact_precision)]
  transfers between devices with their start and end apart: 21 -> 0, of which waited for: 21 -> 0; matrix products, arithmetic and copies ran while one was open for 1% -> 0% of each run, Pallas kernels for 0% -> 0%
where the time goes in v1:
time: 75.6 us; the launch traced here: 75.1 us
  Pallas kernels  60.5 us (80%)
  local copies, waits for them, and re-layouts  13.9 us (18%)
    pallas_call x1, Pallas kernels, shards(): pl.pallas_call(functools.partial(kernel, n_ctx, n_ch), out_shape=(wide, w...  60.5 us
    unnamed x36, local copies, waits for them, and re-layouts  13.9 us

profile of v1, /device:TPU:1, one launch (start us, length us, event | category | flops | bytes accessed | tf_op | source)
XLA Modules:
  0.0 75.1 jit_solution(1298563610443142996)
XLA Ops:
  0.6 0.0 copy-start.11
  0.6 0.0 copy-start.12
  0.7 0.0 copy-start.13
  0.7 0.0 copy-start.14
  0.7 0.8 %copy.21.basis_ref = bf16[128,64]{1,0:T(8,128)(2,1)S(1)} copy(bf16[128,64]{0,1:T(8,128)(2,1)} %param.20) | data formatting | bytes 32768 | tf_op args[4]
  1.5 0.0 copy-done.11
  1.5 0.0 copy-done.12
  1.5 0.0 copy-done.13
  1.6 0.0 copy-done.14
  1.6 0.0 copy-start
  1.6 0.9 %copy-done = f32[2,256,128]{2,1,0:T(8,128)S(1)} copy-done((f32[2,256,128]{2,1,0:T(8,128)S(1)}, f32[2,256,128]{2,1,0:T(8,128)}, u32[]{:S(2)}) %copy-start) | copy-done | bytes 262168
  2.5 0.0 copy-start.1
  2.5 0.9 %copy-done.1 = bf16[256,512]{1,0:T(8,128)(2,1)S(1)} copy-done((bf16[256,512]{1,0:T(8,128)(2,1)S(1)}, bf16[256,512]{1,0:T(8,128)(2,1)}, u32[]{:S(2)}) %copy-start.1) | copy-done | bytes 262168
  3.5 0.0 copy-start.2
  3.5 0.9 %copy-done.2 = bf16[256,512]{1,0:T(8,128)(2,1)S(1)} copy-done((bf16[256,512]{1,0:T(8,128)(2,1)S(1)}, bf16[256,512]{1,0:T(8,128)(2,1)}, u32[]{:S(2)}) %copy-start.2) | copy-done | bytes 262168
  4.4 0.0 copy-start.3
  4.4 0.9 %copy-done.3 = bf16[512,256]{1,0:T(8,128)(2,1)S(1)} copy-done((bf16[512,256]{1,0:T(8,128)(2,1)S(1)}, bf16[512,256]{1,0:T(8,128)(2,1)}, u32[]{:S(2)}) %copy-start.3) | copy-done | bytes 262168
  5.4 0.0 copy-start.4
  5.4 0.9 %copy-done.4 = bf16[512,256]{1,0:T(8,128)(2,1)S(1)} copy-done((bf16[512,256]{1,0:T(8,128)(2,1)S(1)}, bf16[512,256]{1,0:T(8,128)(2,1)}, u32[]{:S(2)}) %copy-start.4) | copy-done | bytes 262168
  6.3 0.0 copy-start.5
  6.3 0.9 %copy-done.5 = bf16[256,256]{1,0:T(8,128)(2,1)S(1)} copy-done((bf16[256,256]{1,0:T(8,128)(2,1)S(1)}, bf16[256,256]{1,0:T(8,128)(2,1)}, u32[]{:S(2)}) %copy-start.5) | copy-done | bytes 131096
  7.2 0.0 copy-start.6
  7.2 0.9 %copy-done.6 = bf16[256,256]{1,0:T(8,128)(2,1)S(1)} copy-done((bf16[256,256]{1,0:T(8,128)(2,1)S(1)}, bf16[256,256]{1,0:T(8,128)(2,1)}, u32[]{:S(2)}) %copy-start.6) | copy-done | bytes 131096
  8.1 0.0 copy-start.7
  8.1 0.8 %copy-done.7 = bf16[128,256]{1,0:T(8,128)(2,1)S(1)} copy-done((bf16[128,256]{1,0:T(8,128)(2,1)S(1)}, bf16[128,256]{1,0:T(8,128)(2,1)}, u32[]{:S(2)}) %copy-start.7) | copy-done | bytes 65560
  9.0 0.0 copy-start.8
  9.0 0.8 %copy-done.8 = bf16[128,256]{1,0:T(8,128)(2,1)S(1)} copy-done((bf16[128,256]{1,0:T(8,128)(2,1)S(1)}, bf16[128,256]{1,0:T(8,128)(2,1)}, u32[]{:S(2)}) %copy-start.8) | copy-done | bytes 65560
  9.8 0.0 copy-start.9
  9.8 0.8 %copy-done.9 = bf16[128,256]{1,0:T(8,128)(2,1)S(1)} copy-done((bf16[128,256]{1,0:T(8,128)(2,1)S(1)}, bf16[128,256]{1,0:T(8,128)(2,1)}, u32[]{:S(2)}) %copy-start.9) | copy-done | bytes 65560
  10.6 0.0 copy-start.10
  10.6 0.8 %copy-done.10 = bf16[128,256]{1,0:T(8,128)(2,1)S(1)} copy-done((bf16[128,256]{1,0:T(8,128)(2,1)S(1)}, bf16[128,256]{1,0:T(8,128)(2,1)}, u32[]{:S(2)}) %copy-start.10) | copy-done | bytes 65560
  11.5 60.5 %shard_map.191 = (bf16[128,256]{1,0:T(8,128)(2,1)S(1)}, bf16[128,256]{1,0:T(8,128)(2,1)S(1)}, bf16[128,256]{1,0:T(8,128)(2,1)S(1)}, bf16[128,256]{1,0:T(8,128)(2,1)S(1)}, f32[2,256]{1,0:T(2,128)S(1)}) custom-call(bf16[128,256]{1,0:T(8,128)(2,1)S(1)} %copy-done.7, bf16[128,256]{1,0:T(8,128)(2,1)S(1)} %copy-done.8, bf16[128,256]{1,0:T(8,128)(2,1)S(1)} %copy-done.9, ...), custom_call_target="tpu_custom_call" | custom-call | tf_op jit(solution)/shard_map/pallas_call | solution.py:288
  72.0 0.6 copy.27
  72.6 0.6 copy.28
  73.2 0.6 copy.29
  73.9 0.6 copy.30
  74.5 0.6 copy.31
Async XLA Ops:
  0.6 0.9 %copy-start.11 = (bf16[64,256]{1,0:T(8,128)(2,1)S(1)}, bf16[64,256]{1,0:T(8,128)(2,1)}, u32[]{:S(2)}) copy-start(bf16[64,256]{1,0:T(8,128)(2,1)} %weight_ref.1) | copy-start | bytes 98308
  0.6 0.9 %copy-start.12 = (f32[256]{0:T(256)S(1)}, f32[256]{0:T(256)}, u32[]{:S(2)}) copy-start(f32[256]{0:T(256)} %param.22) | copy-start | bytes 3076
  0.7 0.9 %copy-start.13 = (f32[256]{0:T(256)S(1)}, f32[256]{0:T(256)}, u32[]{:S(2)}) copy-start(f32[256]{0:T(256)} %param.23) | copy-start | bytes 3076
  0.7 0.9 %copy-start.14 = (f32[256]{0:T(256)S(1)}, f32[256]{0:T(256)}, u32[]{:S(2)}) copy-start(f32[256]{0:T(256)} %param.24) | copy-start | bytes 3076
  1.6 1.0 %copy-start = (f32[2,256,128]{2,1,0:T(8,128)S(1)}, f32[2,256,128]{2,1,0:T(8,128)}, u32[]{:S(2)}) copy-start(f32[2,256,128]{2,1,0:T(8,128)} %constant.20.clone.turns) | copy-start | bytes 786436
  2.5 0.9 %copy-start.1 = (bf16[256,512]{1,0:T(8,128)(2,1)S(1)}, bf16[256,512]{1,0:T(8,128)(2,1)}, u32[]{:S(2)}) copy-start(bf16[256,512]{1,0:T(8,128)(2,1)} %constant.17.clone.back_lo) | copy-start | bytes 786436
  3.5 0.9 %copy-start.2 = (bf16[256,512]{1,0:T(8,128)(2,1)S(1)}, bf16[256,512]{1,0:T(8,128)(2,1)}, u32[]{:S(2)}) copy-start(bf16[256,512]{1,0:T(8,128)(2,1)} %constant.16.clone.back_hi) | copy-start | bytes 786436
  4.4 0.9 %copy-start.3 = (bf16[512,256]{1,0:T(8,128)(2,1)S(1)}, bf16[512,256]{1,0:T(8,128)(2,1)}, u32[]{:S(2)}) copy-start(bf16[512,256]{1,0:T(8,128)(2,1)} %constant.15.clone.outer_lo) | copy-start | bytes 786436
  5.4 0.9 %copy-start.4 = (bf16[512,256]{1,0:T(8,128)(2,1)S(1)}, bf16[512,256]{1,0:T(8,128)(2,1)}, u32[]{:S(2)}) copy-start(bf16[512,256]{1,0:T(8,128)(2,1)} %constant.14.clone.outer_hi) | copy-start | bytes 786436
  6.3 0.9 %copy-start.5 = (bf16[256,256]{1,0:T(8,128)(2,1)S(1)}, bf16[256,256]{1,0:T(8,128)(2,1)}, u32[]{:S(2)}) copy-start(bf16[256,256]{1,0:T(8,128)(2,1)} %constant.19.clone.inner_lo) | copy-start | bytes 393220
  7.2 0.9 %copy-start.6 = (bf16[256,256]{1,0:T(8,128)(2,1)S(1)}, bf16[256,256]{1,0:T(8,128)(2,1)}, u32[]{:S(2)}) copy-start(bf16[256,256]{1,0:T(8,128)(2,1)} %constant.18.clone.inner_hi) | copy-start | bytes 393220
  8.1 0.8 %copy-start.7 = (bf16[128,256]{1,0:T(8,128)(2,1)S(1)}, bf16[128,256]{1,0:T(8,128)(2,1)}, u32[]{:S(2)}) copy-start(bf16[128,256]{1,0:T(8,128)(2,1)} %q_ref.1) | copy-start | bytes 196612
  9.0 0.8 %copy-start.8 = (bf16[128,256]{1,0:T(8,128)(2,1)S(1)}, bf16[128,256]{1,0:T(8,128)(2,1)}, u32[]{:S(2)}) copy-start(bf16[128,256]{1,0:T(8,128)(2,1)} %k_ref.1) | copy-start | bytes 196612
  9.8 0.8 %copy-start.9 = (bf16[128,256]{1,0:T(8,128)(2,1)S(1)}, bf16[128,256]{1,0:T(8,128)(2,1)}, u32[]{:S(2)}) copy-start(bf16[128,256]{1,0:T(8,128)(2,1)} %v_ref.1) | copy-start | bytes 196612
  10.6 0.8 %copy-start.10 = (bf16[128,256]{1,0:T(8,128)(2,1)S(1)}, bf16[128,256]{1,0:T(8,128)(2,1)}, u32[]{:S(2)}) copy-start(bf16[128,256]{1,0:T(8,128)(2,1)} %ct_ref.1) | copy-start | bytes 196612

commit v2 on v1

v2 whole, which is shorter than its diff:
```python
import functools
import math

import jax
import jax.numpy as jnp
import ml_dtypes
import numpy as np
from jax import lax
from jax.experimental import pallas as pl
from jax.experimental.pallas import tpu as pltpu
from jax.sharding import PartitionSpec as P

MESH = pl.DeviceIdType.MESH
F32 = jnp.float32
BF16 = jnp.bfloat16

N_Y, N_Z, N_CORE = 2, 8, 2
N_CTX = N_Y * N_Z * N_CORE


def halves(table):
    high = table.astype(np.float32).astype(ml_dtypes.bfloat16)
    low = (table - high.astype(np.float64)).astype(ml_dtypes.bfloat16)
    return high, low


def transform_tables(blocks, rows, group):
    half = 2 * blocks
    odd = 2 * np.arange(blocks) + 1
    angle = math.pi * odd[:, None] * np.arange(blocks)[None, :] / half
    eye = np.eye(group)
    cos_part = np.kron(np.cos(angle), eye)
    sin_part = np.kron(np.sin(angle), eye)
    outer = np.concatenate([cos_part, -sin_part], 0)
    outer_back = np.concatenate([cos_part.T, -sin_part.T], 1) / (blocks * rows)
    index = np.arange(rows)
    inner_angle = 2.0 * math.pi * (index[:, None] * index[None, :] % rows) / rows
    inner_cos, inner_sin = np.cos(inner_angle), -np.sin(inner_angle)
    inner = np.block([[inner_cos, inner_sin], [-inner_sin, inner_cos]])
    turn = np.repeat(math.pi * odd[:, None] * index[None, :] / (half * rows), group, 0)
    turns = np.stack([np.cos(turn), -np.sin(turn)]).astype(np.float32)
    return np.stack(halves(outer)), np.stack(halves(outer_back)), np.stack(halves(inner)), turns


def split(x):
    high = x.astype(BF16)
    return high, (x - high.astype(F32)).astype(BF16)


def dot(a, b):
    return jnp.dot(a, b, preferred_element_type=F32)


def dot_nt(a, b):
    return lax.dot_general(a, b, (((1,), (1,)), ((), ())), preferred_element_type=F32)


def dot3(a, b):
    return dot(a[0], b[0]) + dot(a[0], b[1]) + dot(a[1], b[0])


def product(a, b):
    return a[0] * b[0] - a[1] * b[1], a[0] * b[1] + a[1] * b[0]


def conj(a):
    return a[0], -a[1]


def kernel(
    n_ch,
    q_hbm, k_hbm, v_hbm, ct_hbm, basis_hbm, weight_hbm, rate_hbm, skip_hbm, gain_hbm,
    outer_hbm, back_hbm, inner_hbm, turns_hbm,
    out_ref, gq_ref, gk_ref, gv_ref, gf_ref,
    q_ref, k_ref, v_ref, ct_ref, basis_ref, weight_ref, rate_ref, skip_ref, gain_ref,
    outer_ref, back_ref, inner_ref, turns,
    send_k, send_g, send_c, send_m, send_y, send_s, send_f,
    recv_k, recv_g, recv_c, recv_m, recv_y, recv_s, recv_f,
    all_basis, rates,
    load_sem, send_sem, recv_sem,
):
    width, rows = send_k.shape
    features = basis_ref.shape[0]
    each = features // N_CTX
    group = width // N_CTX
    full_width = width * n_ch
    me = lax.axis_index("ctx")
    my_ch = lax.axis_index("ch")
    my_y, my_z, my_core = me // (N_Z * N_CORE), me // N_CORE % N_Z, me % N_CORE
    y_mate = (my_y + 1) % N_Y * N_Z * N_CORE + me % (N_Z * N_CORE)
    core_mate = me - my_core + (my_core + 1) % N_CORE

    barrier = pltpu.get_barrier_semaphore()

    def greet_ctx(d, carry):
        to = lax.rem(me + d, N_CTX)
        pl.semaphore_signal(barrier, inc=1, device_id={"ctx": to}, device_id_type=MESH)
        return carry

    def greet_ch(d, carry):
        to = lax.rem(my_ch + d, n_ch)
        pl.semaphore_signal(barrier, inc=1, device_id={"ch": to}, device_id_type=MESH)
        return carry

    lax.fori_loop(1, N_CTX, greet_ctx, 0)
    lax.fori_loop(1, n_ch, greet_ch, 0)

    sources = (
        k_hbm, v_hbm, basis_hbm, weight_hbm, rate_hbm,
        q_hbm, ct_hbm, skip_hbm, gain_hbm, outer_hbm, back_hbm, inner_hbm, turns_hbm,
    )
    targets = (
        k_ref, v_ref, basis_ref, weight_ref, rate_ref,
        q_ref, ct_ref, skip_ref, gain_ref, outer_ref, back_ref, inner_ref, turns,
    )
    loads = [
        pltpu.make_async_copy(source, target, load_sem.at[at])
        for at, (source, target) in enumerate(zip(sources, targets))
    ]
    for load in loads:
        load.start()

    def peer(d):
        step, corner = d // 4, d % 4
        away = N_Z // 2 + (step + 1) // 2 * (step % 2 * 2 - 1)
        y = (my_y + 1 - corner // 2) % N_Y
        core = (my_core + 1 - corner % 2) % N_CORE
        return (y * N_Z + (my_z + away) % N_Z) * N_CORE + core

    def exchange(slot, src, dst):
        mine = pl.ds(pl.multiple_of(me * group, group), group)

        def step(d, carry):
            to = peer(d)
            pltpu.make_async_remote_copy(
                src_ref=src.at[pl.ds(pl.multiple_of(to * group, group), group)],
                dst_ref=dst.at[mine],
                send_sem=send_sem.at[slot],
                recv_sem=recv_sem.at[slot],
                device_id={"ctx": to},
                device_id_type=MESH,
            ).start()
            return carry

        lax.fori_loop(0, N_CTX - 1, step, 0)
        dst[mine] = src[mine]

    def wait_for(slot, ref, extent, axis, to):
        return pltpu.make_async_remote_copy(
            src_ref=ref.at[extent],
            dst_ref=ref.at[extent],
            send_sem=send_sem.at[slot],
            recv_sem=recv_sem.at[slot],
            device_id={axis: to},
            device_id_type=MESH,
        )

    def blocks_wait(slot, ref):
        return wait_for(slot, ref, pl.ds(0, (N_CTX - 1) * group), "ctx", core_mate)

    def turned(real, imag):
        cos_w, sin_w = turns[0], turns[1]
        return jnp.concatenate([real * cos_w - imag * sin_w, real * sin_w + imag * cos_w], 1)

    def forward(block):
        first = dot3((outer_ref[0], outer_ref[1]), split(block))
        parts = turned(first[:width], first[width:])
        spectrum = dot3(split(parts), (inner_ref[0], inner_ref[1]))
        return spectrum[:, :rows], spectrum[:, rows:]

    def inverse(conjugates):
        stacked = jnp.concatenate([jnp.concatenate(pair, 1) for pair in conjugates], 0)
        first = dot3(split(stacked), (inner_ref[0], inner_ref[1]))
        columns = []
        for at in range(len(conjugates)):
            part = first[at * width : (at + 1) * width]
            z = turned(part[:, :rows], part[:, rows:])
            columns.append(jnp.concatenate([z[:, :rows], -z[:, rows:]], 0))
        return dot3((back_ref[0], back_ref[1]), split(jnp.concatenate(columns, 1)))

    for load in loads[:5]:
        load.wait()
    rate = jnp.broadcast_to(rate_ref[...], (rows, width)).T
    rates[...] = rate
    lane = lax.broadcasted_iota(jnp.int32, (width, rows), 1)
    decay = jnp.exp(-rate * (me * rows + lane).astype(F32))
    weight = weight_ref[...].astype(F32).T.astype(BF16)
    send_k[...] = dot(weight, basis_ref[...]) * decay
    keys = k_ref[...].astype(F32)
    values = v_ref[...].astype(F32)
    gated = (keys * values).T
    send_g[...] = gated
    all_basis[me] = basis_ref[...].astype(F32)

    pl.semaphore_wait(barrier, N_CTX + n_ch - 2)
    exchange(0, send_k, recv_k)
    exchange(1, send_g, recv_g)

    def spread(d, carry):
        away = N_Z // 2 + (d + 1) // 2 * (d % 2 * 2 - 1)
        to = me - my_z * N_CORE + (my_z + away) % N_Z * N_CORE
        pltpu.make_async_remote_copy(
            src_ref=all_basis.at[me],
            dst_ref=all_basis.at[me],
            send_sem=send_sem.at[4],
            recv_sem=recv_sem.at[4],
            device_id={"ctx": to},
            device_id_type=MESH,
        ).start()
        return carry

    lax.fori_loop(0, N_Z - 1, spread, 0)

    for load in loads[5:]:
        load.wait()
    queries = q_ref[...].astype(F32).T
    scaled = (ct_ref[...].astype(F32) * gain_ref[...]).T
    skip = jnp.broadcast_to(skip_ref[...], (rows, width)).T
    gain = gain_ref[...]

    blocks_wait(0, recv_k).wait_recv()
    kernel_spec = forward(recv_k[...])
    blocks_wait(1, recv_g).wait_recv()
    gated_spec = forward(recv_g[...])
    send_c[...] = inverse([conj(product(gated_spec, kernel_spec))])
    exchange(2, send_c, recv_c)

    own_rate = rates[pl.ds(pl.multiple_of(me * group, group), group)]
    row = lax.broadcasted_iota(jnp.int32, (width, rows), 0)
    own_decay = jnp.exp(
        -jnp.concatenate([own_rate] * N_CTX, 0) * (row // group * rows + lane).astype(F32)
    )

    blocks_wait(2, recv_c).wait_recv()
    mixed = recv_c[...] + skip * gated
    signal = queries * mixed
    send_s[0:1] = jnp.sum(signal * signal, axis=0, keepdims=True)
    send_s[1:2] = jnp.sum(signal * scaled, axis=0, keepdims=True)

    def share(d, carry):
        to = lax.rem(my_ch + d, n_ch)
        pltpu.make_async_remote_copy(
            src_ref=send_s,
            dst_ref=recv_s.at[my_ch],
            send_sem=send_sem.at[3],
            recv_sem=recv_sem.at[3],
            device_id={"ch": to},
            device_id_type=MESH,
        ).start()
        return carry

    lax.fori_loop(1, n_ch, share, 0)
    recv_s[my_ch] = send_s[...]

    wait_for(4, all_basis, pl.ds(0, N_Z - 1), "ctx", core_mate).wait_recv()
    for z in range(N_Z):
        slot = my_y * N_Z * N_CORE + z * N_CORE + my_core
        pltpu.make_async_remote_copy(
            src_ref=all_basis.at[slot],
            dst_ref=all_basis.at[slot],
            send_sem=send_sem.at[8],
            recv_sem=recv_sem.at[8],
            device_id={"ctx": y_mate},
            device_id_type=MESH,
        ).start()

    sums_wait = wait_for(3, recv_s, pl.ds(0, n_ch - 1), "ch", lax.rem(my_ch + 1, n_ch))
    sums_wait.wait_recv()
    sums = jnp.sum(recv_s[...], axis=0)
    inv_rms = lax.rsqrt(sums[0:1] / full_width + 1e-06)
    pull = inv_rms * inv_rms * inv_rms * sums[1:2] / full_width
    grad_signal = inv_rms * scaled - signal * pull
    grad_mixed = grad_signal * queries
    send_m[...] = grad_mixed
    exchange(5, send_m, recv_m)

    out_ref[...] = ((signal * inv_rms).T * gain).astype(BF16)
    gq_ref[...] = (grad_signal * mixed).T.astype(BF16)

    wait_for(8, all_basis, pl.ds(0, N_Z), "ctx", y_mate).wait_recv()
    for at in range(N_Y * N_Z):
        slot = at * N_CORE + my_core
        pltpu.make_async_remote_copy(
            src_ref=all_basis.at[slot],
            dst_ref=all_basis.at[slot],
            send_sem=send_sem.at[9],
            recv_sem=recv_sem.at[9],
            device_id={"ctx": core_mate},
            device_id_type=MESH,
        ).start()

    blocks_wait(5, recv_m).wait_recv()
    grad_spec = conj(forward(recv_m[...]))
    both = inverse([product(kernel_spec, grad_spec), product(gated_spec, grad_spec)])
    send_y[...] = both[:, :rows]
    exchange(6, send_y, recv_y)

    wait_for(9, all_basis, pl.ds(0, N_Y * N_Z), "ctx", core_mate).wait_recv()
    high, low = split(both[:, rows:] * own_decay)
    total = jnp.zeros((features, 2 * group), F32)
    for at in range(N_CTX):
        take = slice(at * group, (at + 1) * group)
        pair = jnp.concatenate([high[take].astype(F32), low[take].astype(F32)], 0).astype(BF16)
        total += dot_nt(all_basis[at].astype(BF16), pair)
    total = total[:, :group] + total[:, group:]
    own_filter = jnp.concatenate([total, jnp.zeros((features, rows - group), F32)], 1)
    own_filter = pltpu.roll(own_filter, me * group % rows, 1)
    for at in range(N_CTX):
        send_f[at] = own_filter[at * each : (at + 1) * each]

    def scatter(d, carry):
        to = peer(d)
        pltpu.make_async_remote_copy(
            src_ref=send_f.at[to],
            dst_ref=recv_f.at[me],
            send_sem=send_sem.at[7],
            recv_sem=recv_sem.at[7],
            device_id={"ctx": to},
            device_id_type=MESH,
        ).start()
        return carry

    lax.fori_loop(0, N_CTX - 1, scatter, 0)
    recv_f[me] = send_f[me]

    blocks_wait(6, recv_y).wait_recv()
    grad_gated = (recv_y[...] + skip * grad_mixed).T
    gk_ref[...] = (grad_gated * values).astype(BF16)
    gv_ref[...] = (grad_gated * keys).astype(BF16)

    filter_wait = wait_for(7, recv_f, pl.ds(0, N_CTX - 1), "ctx", core_mate)
    filter_wait.wait_recv()
    per = rows // group
    for at in range(width // rows):
        gf_ref[:, at * rows : (at + 1) * rows] = jnp.sum(recv_f[at * per : (at + 1) * per], axis=0)

    blocks_wait(0, send_k).wait_send()
    blocks_wait(1, send_g).wait_send()
    blocks_wait(2, send_c).wait_send()
    blocks_wait(5, send_m).wait_send()
    blocks_wait(6, send_y).wait_send()
    sums_wait.wait_send()
    filter_wait.wait_send()
    wait_for(4, all_basis, pl.ds(0, N_Z - 1), "ctx", core_mate).wait_send()
    wait_for(8, all_basis, pl.ds(0, N_Z), "ctx", y_mate).wait_send()
    wait_for(9, all_basis, pl.ds(0, N_Y * N_Z), "ctx", core_mate).wait_send()


def store(*refs):
    count = len(refs) // 2
    copies = [
        pltpu.make_async_copy(refs[at], refs[count + at], refs[-1].at[at]) for at in range(count)
    ]
    for copy in copies:
        copy.start()
    for copy in copies:
        copy.wait()


def solution(mesh):
    n_ctx, n_ch = mesh.shape["ctx"], mesh.shape["ch"]
    assert n_ctx == N_CTX

    def shards(query, key, value, cotangent, basis, weight, rate, skip, gain):
        rows, width = query.shape
        features = basis.shape[1]
        each = features // n_ctx
        tables = transform_tables(n_ctx, rows, width // n_ctx)
        operands = (
            query, key, value, cotangent, basis.T, weight,
            rate[None, :], skip[None, :], gain[None, :],
            *(jnp.asarray(table) for table in tables),
        )
        inside = pl.BlockSpec(memory_space=pltpu.VMEM)
        outside = pl.BlockSpec(memory_space=pltpu.HBM)
        wide = jax.ShapeDtypeStruct((rows, width), BF16)
        results = (wide, wide, wide, wide, jax.ShapeDtypeStruct((each, width), F32))
        slots = [pltpu.VMEM((width, rows), F32)] * 5
        last = [pltpu.VMEM((n_ctx, each, rows), F32)]
        computed = pl.pallas_call(
            functools.partial(kernel, n_ch),
            out_shape=results,
            in_specs=[outside] * len(operands),
            out_specs=(inside,) * 5,
            scratch_shapes=[
                *(pltpu.VMEM(operand.shape, operand.dtype) for operand in operands),
                *slots,
                pltpu.VMEM((2, rows), F32),
                *last,
                *slots,
                pltpu.VMEM((n_ch, 2, rows), F32),
                *last,
                pltpu.VMEM((n_ctx, features, rows), F32),
                pltpu.VMEM((width, rows), F32),
                pltpu.SemaphoreType.DMA((len(operands),)),
                pltpu.SemaphoreType.DMA((10,)),
                pltpu.SemaphoreType.DMA((10,)),
            ],
            compiler_params=pltpu.CompilerParams(
                collective_id=0, has_side_effects=True, vmem_limit_bytes=60 * 1024 * 1024
            ),
        )(*operands)
        return pl.pallas_call(
            store,
            out_shape=results,
            in_specs=[inside] * 5,
            out_specs=(outside,) * 5,
            scratch_shapes=[pltpu.SemaphoreType.DMA((5,))],
        )(*computed)

    return jax.shard_map(
        shards,
        mesh=mesh,
        in_specs=(
            P("ctx", "ch"), P("ctx", "ch"), P("ctx", "ch"), P("ctx", "ch"),
            P("ctx", None), P(None, "ch"), P("ch"), P("ch"), P("ch"),
        ),
        out_specs=(P("ctx", "ch"),) * 5,
        check_vma=False,
    )
```

time: 75.6 us -> 57.6 us (0.76)
  local copies, waits for them, and re-layouts: 13.9 us -> 0 us
  Pallas kernels: 60.5 us -> 56.7 us
    unnamed x36 -> x0, local copies, waits for them, and re-layouts: 13.9 us -> none
    pallas_call x1 -> x2, Pallas kernels: 60.5 us -> 56.7 us  [the longest x1 55.1 us: shards(): pl.pallas_call(functools.partial(kernel, n_ch), out_shape=results, in_spe...]
where the time goes in v2:
time: 57.6 us; the launch traced here: 57.4 us
  Pallas kernels  56.7 us (98%)
  between operations  0.64 us (1%)
    pallas_call x1, Pallas kernels, shards(): pl.pallas_call(functools.partial(kernel, n_ch), out_shape=results, in_spe...  55.1 us
    pallas_call x1, Pallas kernels, shards(): pl.pallas_call(store, out_shape=results, in_specs=[inside] * 5, out_specs...  1.68 us

profile of v2, /device:TPU:1, one launch (start us, length us, event | category | flops | bytes accessed | tf_op | source)
XLA Modules:
  0.0 57.4 jit_solution(6217192093615397373)
XLA Ops:
  0.6 55.1 %shard_map.164 = (bf16[128,256]{1,0:T(8,128)(2,1)}, bf16[128,256]{1,0:T(8,128)(2,1)}, bf16[128,256]{1,0:T(8,128)(2,1)}, bf16[128,256]{1,0:T(8,128)(2,1)}, f32[2,256]{1,0:T(2,128)}) custom-call(bf16[128,256]{1,0:T(8,128)(2,1)} %q_hbm.1, bf16[128,256]{1,0:T(8,128)(2,1)} %k_hbm.1, bf16[128,256]{1,0:T(8,128)(2,1)} %v_hbm.1, bf16[128,256]{1,0:T(8,128)(2,1)} %ct_hbm.1, ...), custom_call_target="tpu_custom_call" | custom-call | tf_op jit(solution)/shard_map/pallas_call | solution.py:380
  55.7 1.7 %shard_map.165 = (bf16[128,256]{1,0:T(8,128)(2,1)}, bf16[128,256]{1,0:T(8,128)(2,1)}, bf16[128,256]{1,0:T(8,128)(2,1)}, bf16[128,256]{1,0:T(8,128)(2,1)}, f32[2,256]{1,0:T(2,128)}) custom-call(bf16[128,256]{1,0:T(8,128)(2,1)} %get-tuple-element.10.refs_0_, bf16[128,256]{1,0:T(8,128)(2,1)} %get-tuple-element.11.refs_1_, ...), custom_call_target="tpu_custom_call" | custom-call | tf_op jit(solution)/shard_map/pallas_call | solution.py:403

commit v3 on v2

--- a/solution.py
+++ b/solution.py
@@ -59,6 +59,12 @@
     return dot(a[0], b[0]) + dot(a[0], b[1]) + dot(a[1], b[0])
 
 
+def dot3_wide(a, b):
+    columns = b[0].shape[1]
+    both = dot(a[0], jnp.concatenate(b, 1))
+    return both[:, :columns] + both[:, columns:] + dot(a[1], b[0])
+
+
 def product(a, b):
     return a[0] * b[0] - a[1] * b[1], a[0] * b[1] + a[1] * b[0]
 
@@ -76,7 +82,7 @@
     outer_ref, back_ref, inner_ref, turns,
     send_k, send_g, send_c, send_m, send_y, send_s, send_f,
     recv_k, recv_g, recv_c, recv_m, recv_y, recv_s, recv_f,
-    all_basis, rates,
+    all_basis, rates, wide_basis, own_grad,
     load_sem, send_sem, recv_sem,
 ):
     width, rows = send_k.shape
@@ -90,20 +96,23 @@
     y_mate = (my_y + 1) % N_Y * N_Z * N_CORE + me % (N_Z * N_CORE)
     core_mate = me - my_core + (my_core + 1) % N_CORE
 
+    peers = []
+    for dy in (1, 0):
+        for dc in (1, 0):
+            corner = lax.rem(my_y + dy, N_Y) * (N_Z * N_CORE) + lax.rem(my_core + dc, N_CORE)
+            for dz in (4, 3, 5, 2, 6, 1, 7, 0):
+                if (dy, dz, dc) != (0, 0, 0):
+                    peers.append(corner + lax.rem(my_z + dz, N_Z) * N_CORE)
+    half = N_CTX // 2
+    other_y = lax.rem(my_y + 1, N_Y)
+    ch_peers = [lax.rem(my_ch + d, n_ch) for d in range(1, n_ch)]
+
     barrier = pltpu.get_barrier_semaphore()
 
-    def greet_ctx(d, carry):
-        to = lax.rem(me + d, N_CTX)
+    for to in peers:
         pl.semaphore_signal(barrier, inc=1, device_id={"ctx": to}, device_id_type=MESH)
-        return carry
-
-    def greet_ch(d, carry):
-        to = lax.rem(my_ch + d, n_ch)
+    for to in ch_peers:
         pl.semaphore_signal(barrier, inc=1, device_id={"ch": to}, device_id_type=MESH)
-        return carry
-
-    lax.fori_loop(1, N_CTX, greet_ctx, 0)
-    lax.fori_loop(1, n_ch, greet_ch, 0)
 
     sources = (
         k_hbm, v_hbm, basis_hbm, weight_hbm, rate_hbm,
@@ -120,18 +129,9 @@
     for load in loads:
         load.start()
 
-    def peer(d):
-        step, corner = d // 4, d % 4
-        away = N_Z // 2 + (step + 1) // 2 * (step % 2 * 2 - 1)
-        y = (my_y + 1 - corner // 2) % N_Y
-        core = (my_core + 1 - corner % 2) % N_CORE
-        return (y * N_Z + (my_z + away) % N_Z) * N_CORE + core
-
-    def exchange(slot, src, dst):
+    def exchange(slot, src, dst, to_peers):
         mine = pl.ds(pl.multiple_of(me * group, group), group)
-
-        def step(d, carry):
-            to = peer(d)
+        for to in to_peers:
             pltpu.make_async_remote_copy(
                 src_ref=src.at[pl.ds(pl.multiple_of(to * group, group), group)],
                 dst_ref=dst.at[mine],
@@ -140,9 +140,21 @@
                 device_id={"ctx": to},
                 device_id_type=MESH,
             ).start()
-            return carry
-
-        lax.fori_loop(0, N_CTX - 1, step, 0)
+
+    def planes_in_order(y, act):
+        for z in range(N_Z):
+            for core in (lax.rem(my_core + 1, N_CORE), my_core):
+                to = (y * N_Z + z) * N_CORE + core
+
+                @pl.when(to != me)
+                def _():
+                    act(to)
+
+    def give_back(slot, src, dst, to):
+        exchange(slot, src, dst, [to])
+
+    def keep_own(src, dst):
+        mine = pl.ds(pl.multiple_of(me * group, group), group)
         dst[mine] = src[mine]
 
     def wait_for(slot, ref, extent, axis, to):
@@ -163,7 +175,7 @@
         return jnp.concatenate([real * cos_w - imag * sin_w, real * sin_w + imag * cos_w], 1)
 
     def forward(block):
-        first = dot3((outer_ref[0], outer_ref[1]), split(block))
+        first = dot3_wide((outer_ref[0], outer_ref[1]), split(block))
         parts = turned(first[:width], first[width:])
         spectrum = dot3(split(parts), (inner_ref[0], inner_ref[1]))
         return spectrum[:, :rows], spectrum[:, rows:]
@@ -176,7 +188,13 @@
             part = first[at * width : (at + 1) * width]
             z = turned(part[:, :rows], part[:, rows:])
             columns.append(jnp.concatenate([z[:, :rows], -z[:, rows:]], 0))
-        return dot3((back_ref[0], back_ref[1]), split(jnp.concatenate(columns, 1)))
+        return split(jnp.concatenate(columns, 1))
+
+    side = width // N_Y
+
+    def blocks_of(y, columns, multiply):
+        take = pl.ds(pl.multiple_of(y * side, side), side)
+        return take, multiply((back_ref[0, take], back_ref[1, take]), columns)
 
     for load in loads[:5]:
         load.wait()
@@ -193,23 +211,25 @@
     all_basis[me] = basis_ref[...].astype(F32)
 
     pl.semaphore_wait(barrier, N_CTX + n_ch - 2)
-    exchange(0, send_k, recv_k)
-    exchange(1, send_g, recv_g)
-
-    def spread(d, carry):
-        away = N_Z // 2 + (d + 1) // 2 * (d % 2 * 2 - 1)
-        to = me - my_z * N_CORE + (my_z + away) % N_Z * N_CORE
+    exchange(0, send_k, recv_k, peers)
+    exchange(1, send_g, recv_g, peers)
+    keep_own(send_k, recv_k)
+    keep_own(send_g, recv_g)
+
+    def pass_on(slot, origin, away):
+        at = me + (lax.rem(my_z + origin, N_Z) - my_z) * N_CORE
+        to = me + (lax.rem(my_z + away, N_Z) - my_z) * N_CORE
         pltpu.make_async_remote_copy(
-            src_ref=all_basis.at[me],
-            dst_ref=all_basis.at[me],
-            send_sem=send_sem.at[4],
-            recv_sem=recv_sem.at[4],
+            src_ref=all_basis.at[at],
+            dst_ref=all_basis.at[at],
+            send_sem=send_sem.at[slot],
+            recv_sem=recv_sem.at[slot],
             device_id={"ctx": to},
             device_id_type=MESH,
         ).start()
-        return carry
-
-    lax.fori_loop(0, N_Z - 1, spread, 0)
+
+    for away in (2, N_Z - 2, 1, N_Z - 1):
+        pass_on(4, 0, away)
 
     for load in loads[5:]:
         load.wait()
@@ -222,8 +242,17 @@
     kernel_spec = forward(recv_k[...])
     blocks_wait(1, recv_g).wait_recv()
     gated_spec = forward(recv_g[...])
-    send_c[...] = inverse([conj(product(gated_spec, kernel_spec))])
-    exchange(2, send_c, recv_c)
+    columns = inverse([conj(product(gated_spec, kernel_spec))])
+    for y, some in ((other_y, peers[:half]), (my_y, peers[half:])):
+        take, blocks = blocks_of(y, columns, dot3_wide)
+        send_c[take] = blocks
+        exchange(2, send_c, recv_c, some)
+    keep_own(send_c, recv_c)
+
+    wait_for(4, all_basis, pl.ds(0, 4), "ctx", core_mate).wait_recv()
+    pass_on(10, N_Z - 2, 2)
+    pass_on(10, N_Z - 2, 1)
+    pass_on(10, 2, N_Z - 1)
 
     own_rate = rates[pl.ds(pl.multiple_of(me * group, group), group)]
     row = lax.broadcasted_iota(jnp.int32, (width, rows), 0)
@@ -237,8 +266,7 @@
     send_s[0:1] = jnp.sum(signal * signal, axis=0, keepdims=True)
     send_s[1:2] = jnp.sum(signal * scaled, axis=0, keepdims=True)
 
-    def share(d, carry):
-        to = lax.rem(my_ch + d, n_ch)
+    for to in ch_peers:
         pltpu.make_async_remote_copy(
             src_ref=send_s,
             dst_ref=recv_s.at[my_ch],
@@ -247,12 +275,10 @@
             device_id={"ch": to},
             device_id_type=MESH,
         ).start()
-        return carry
-
-    lax.fori_loop(1, n_ch, share, 0)
+
     recv_s[my_ch] = send_s[...]
 
-    wait_for(4, all_basis, pl.ds(0, N_Z - 1), "ctx", core_mate).wait_recv()
+    wait_for(10, all_basis, pl.ds(0, 3), "ctx", core_mate).wait_recv()
     for z in range(N_Z):
         slot = my_y * N_Z * N_CORE + z * N_CORE + my_core
         pltpu.make_async_remote_copy(
@@ -272,7 +298,8 @@
     grad_signal = inv_rms * scaled - signal * pull
     grad_mixed = grad_signal * queries
     send_m[...] = grad_mixed
-    exchange(5, send_m, recv_m)
+    exchange(5, send_m, recv_m, peers)
+    keep_own(send_m, recv_m)
 
     out_ref[...] = ((signal * inv_rms).T * gain).astype(BF16)
     gq_ref[...] = (grad_signal * mixed).T.astype(BF16)
@@ -289,27 +316,33 @@
             device_id_type=MESH,
         ).start()
 
+    wait_for(9, all_basis, pl.ds(0, N_Y * N_Z), "ctx", core_mate).wait_recv()
+    for at in range(N_CTX):
+        wide_basis[:, at * rows : (at + 1) * rows] = all_basis[at].astype(BF16)
+
     blocks_wait(5, recv_m).wait_recv()
     grad_spec = conj(forward(recv_m[...]))
-    both = inverse([product(kernel_spec, grad_spec), product(gated_spec, grad_spec)])
-    send_y[...] = both[:, :rows]
-    exchange(6, send_y, recv_y)
-
-    wait_for(9, all_basis, pl.ds(0, N_Y * N_Z), "ctx", core_mate).wait_recv()
-    high, low = split(both[:, rows:] * own_decay)
-    total = jnp.zeros((features, 2 * group), F32)
-    for at in range(N_CTX):
-        take = slice(at * group, (at + 1) * group)
-        pair = jnp.concatenate([high[take].astype(F32), low[take].astype(F32)], 0).astype(BF16)
-        total += dot_nt(all_basis[at].astype(BF16), pair)
+    columns = inverse([product(kernel_spec, grad_spec), product(gated_spec, grad_spec)])
+    for y in (other_y, my_y):
+        take, blocks = blocks_of(y, columns, dot3)
+        send_y[take] = blocks[:, :rows]
+        planes_in_order(y, functools.partial(give_back, 6, send_y, recv_y))
+        own_grad[take] = blocks[:, rows:]
+    keep_own(send_y, recv_y)
+
+    high, low = (part.astype(F32) for part in split(own_grad[...] * own_decay))
+    pairs = [
+        jnp.concatenate([part[at * group : (at + 1) * group] for part in (high, low)], 0)
+        for at in range(N_CTX)
+    ]
+    total = dot_nt(wide_basis[...], jnp.concatenate(pairs, 1).astype(BF16))
     total = total[:, :group] + total[:, group:]
     own_filter = jnp.concatenate([total, jnp.zeros((features, rows - group), F32)], 1)
     own_filter = pltpu.roll(own_filter, me * group % rows, 1)
     for at in range(N_CTX):
         send_f[at] = own_filter[at * each : (at + 1) * each]
 
-    def scatter(d, carry):
-        to = peer(d)
+    def give_filter(to):
         pltpu.make_async_remote_copy(
             src_ref=send_f.at[to],
             dst_ref=recv_f.at[me],
@@ -318,9 +351,9 @@
             device_id={"ctx": to},
             device_id_type=MESH,
         ).start()
-        return carry
-
-    lax.fori_loop(0, N_CTX - 1, scatter, 0)
+
+    for y in (other_y, my_y):
+        planes_in_order(y, give_filter)
     recv_f[me] = send_f[me]
 
     blocks_wait(6, recv_y).wait_recv()
@@ -341,7 +374,8 @@
     blocks_wait(6, send_y).wait_send()
     sums_wait.wait_send()
     filter_wait.wait_send()
-    wait_for(4, all_basis, pl.ds(0, N_Z - 1), "ctx", core_mate).wait_send()
+    wait_for(4, all_basis, pl.ds(0, 4), "ctx", core_mate).wait_send()
+    wait_for(10, all_basis, pl.ds(0, 3), "ctx", core_mate).wait_send()
     wait_for(8, all_basis, pl.ds(0, N_Z), "ctx", y_mate).wait_send()
     wait_for(9, all_basis, pl.ds(0, N_Y * N_Z), "ctx", core_mate).wait_send()
 
@@ -392,9 +426,11 @@
                 *last,
                 pltpu.VMEM((n_ctx, features, rows), F32),
                 pltpu.VMEM((width, rows), F32),
+                pltpu.VMEM((features, n_ctx * rows), BF16),
+                pltpu.VMEM((width, rows), F32),
                 pltpu.SemaphoreType.DMA((len(operands),)),
-                pltpu.SemaphoreType.DMA((10,)),
-                pltpu.SemaphoreType.DMA((10,)),
+                pltpu.SemaphoreType.DMA((11,)),
+                pltpu.SemaphoreType.DMA((11,)),
             ],
             compiler_params=pltpu.CompilerParams(
                 collective_id=0, has_side_effects=True, vmem_limit_bytes=60 * 1024 * 1024

time: 57.6 us -> 56 us (0.972)
  Pallas kernels: 56.7 us -> 55.2 us
    pallas_call x1, Pallas kernels: 55.1 us -> 53.5 us  [shards(): pl.pallas_call(functools.partial(kernel, n_ch), out_shape=results, in_spe...]
where the time goes in v3:
time: 56 us; the launch traced here: 55.8 us
  Pallas kernels  55.2 us (99%)
  between operations  0.64 us (1%)
    pallas_call x1, Pallas kernels, shards(): pl.pallas_call(functools.partial(kernel, n_ch), out_shape=results, in_spe...  53.5 us
    pallas_call x1, Pallas kernels, shards(): pl.pallas_call(store, out_shape=results, in_specs=[inside] * 5, out_specs...  1.68 us

profile of v3, /device:TPU:1, one launch (start us, length us, event | category | flops | bytes accessed | tf_op | source)
XLA Modules:
  0.0 55.8 jit_solution(1150186177247897837)
XLA Ops:
  0.6 53.5 %shard_map.164 = (bf16[128,256]{1,0:T(8,128)(2,1)}, bf16[128,256]{1,0:T(8,128)(2,1)}, bf16[128,256]{1,0:T(8,128)(2,1)}, bf16[128,256]{1,0:T(8,128)(2,1)}, f32[2,256]{1,0:T(2,128)}) custom-call(bf16[128,256]{1,0:T(8,128)(2,1)} %q_hbm.1, bf16[128,256]{1,0:T(8,128)(2,1)} %k_hbm.1, bf16[128,256]{1,0:T(8,128)(2,1)} %v_hbm.1, bf16[128,256]{1,0:T(8,128)(2,1)} %ct_hbm.1, ...), custom_call_target="tpu_custom_call" | custom-call | tf_op jit(solution)/shard_map/pallas_call | solution.py:414
  54.2 1.7 %shard_map.165 = (bf16[128,256]{1,0:T(8,128)(2,1)}, bf16[128,256]{1,0:T(8,128)(2,1)}, bf16[128,256]{1,0:T(8,128)(2,1)}, bf16[128,256]{1,0:T(8,128)(2,1)}, f32[2,256]{1,0:T(2,128)}) custom-call(bf16[128,256]{1,0:T(8,128)(2,1)} %get-tuple-element.10.refs_0_, bf16[128,256]{1,0:T(8,128)(2,1)} %get-tuple-element.11.refs_1_, ...), custom_call_target="tpu_custom_call" | custom-call | tf_op jit(solution)/shard_map/pallas_call | solution.py:439

commit v4 on v3

--- a/solution.py
+++ b/solution.py
@@ -16,6 +16,7 @@
 
 N_Y, N_Z, N_CORE = 2, 8, 2
 N_CTX = N_Y * N_Z * N_CORE
+N_CH_Y, N_CH_X = 4, 4
 
 
 def halves(table):
@@ -80,12 +81,12 @@
     out_ref, gq_ref, gk_ref, gv_ref, gf_ref,
     q_ref, k_ref, v_ref, ct_ref, basis_ref, weight_ref, rate_ref, skip_ref, gain_ref,
     outer_ref, back_ref, inner_ref, turns,
-    send_k, send_g, send_c, send_m, send_y, send_s, send_f,
-    recv_k, recv_g, recv_c, recv_m, recv_y, recv_s, recv_f,
+    send_kg, send_c, send_m, send_y, send_s, send_f,
+    recv_kg, recv_c, recv_m, recv_y, recv_s, recv_f,
     all_basis, rates, wide_basis, own_grad,
     load_sem, send_sem, recv_sem,
 ):
-    width, rows = send_k.shape
+    width, rows = send_c.shape
     features = basis_ref.shape[0]
     each = features // N_CTX
     group = width // N_CTX
@@ -105,7 +106,14 @@
                     peers.append(corner + lax.rem(my_z + dz, N_Z) * N_CORE)
     half = N_CTX // 2
     other_y = lax.rem(my_y + 1, N_Y)
-    ch_peers = [lax.rem(my_ch + d, n_ch) for d in range(1, n_ch)]
+    far_first = sorted(
+        ((dy, dx) for dy in range(N_CH_Y) for dx in range(N_CH_X) if (dy, dx) != (0, 0)),
+        key=lambda d: -2 * min(d[0], N_CH_Y - d[0]) - min(d[1], N_CH_X - d[1]),
+    )
+    ch_peers = [
+        lax.rem(my_ch // N_CH_X + dy, N_CH_Y) * N_CH_X + lax.rem(my_ch % N_CH_X + dx, N_CH_X)
+        for dy, dx in far_first
+    ]
 
     barrier = pltpu.get_barrier_semaphore()
 
@@ -203,18 +211,25 @@
     lane = lax.broadcasted_iota(jnp.int32, (width, rows), 1)
     decay = jnp.exp(-rate * (me * rows + lane).astype(F32))
     weight = weight_ref[...].astype(F32).T.astype(BF16)
-    send_k[...] = dot(weight, basis_ref[...]) * decay
+    filter_block = dot(weight, basis_ref[...]) * decay
+    send_kg[:, :group] = filter_block.reshape(N_CTX, group, rows)
     keys = k_ref[...].astype(F32)
     values = v_ref[...].astype(F32)
     gated = (keys * values).T
-    send_g[...] = gated
+    send_kg[:, group:] = gated.reshape(N_CTX, group, rows)
     all_basis[me] = basis_ref[...].astype(F32)
 
     pl.semaphore_wait(barrier, N_CTX + n_ch - 2)
-    exchange(0, send_k, recv_k, peers)
-    exchange(1, send_g, recv_g, peers)
-    keep_own(send_k, recv_k)
-    keep_own(send_g, recv_g)
+    for to in peers:
+        pltpu.make_async_remote_copy(
+            src_ref=send_kg.at[to],
+            dst_ref=recv_kg.at[me],
+            send_sem=send_sem.at[0],
+            recv_sem=recv_sem.at[0],
+            device_id={"ctx": to},
+            device_id_type=MESH,
+        ).start()
+    recv_kg[me] = send_kg[me]
 
     def pass_on(slot, origin, away):
         at = me + (lax.rem(my_z + origin, N_Z) - my_z) * N_CORE
@@ -238,10 +253,17 @@
     skip = jnp.broadcast_to(skip_ref[...], (rows, width)).T
     gain = gain_ref[...]
 
-    blocks_wait(0, recv_k).wait_recv()
-    kernel_spec = forward(recv_k[...])
-    blocks_wait(1, recv_g).wait_recv()
-    gated_spec = forward(recv_g[...])
+    first_wait = wait_for(0, recv_kg, pl.ds(0, N_CTX - 1), "ctx", core_mate)
+    first_wait.wait_recv()
+    arrivals = [recv_kg[:, at : at + group].reshape(width, rows) for at in (0, group)]
+    both_first = dot3((outer_ref[0], outer_ref[1]), split(jnp.concatenate(arrivals, 1)))
+    turned_both = [
+        turned(both_first[:width, at : at + rows], both_first[width:, at : at + rows])
+        for at in (0, rows)
+    ]
+    spectra = dot3(split(jnp.concatenate(turned_both, 0)), (inner_ref[0], inner_ref[1]))
+    kernel_spec = spectra[:width, :rows], spectra[:width, rows:]
+    gated_spec = spectra[width:, :rows], spectra[width:, rows:]
     columns = inverse([conj(product(gated_spec, kernel_spec))])
     for y, some in ((other_y, peers[:half]), (my_y, peers[half:])):
         take, blocks = blocks_of(y, columns, dot3_wide)
@@ -367,8 +389,7 @@
     for at in range(width // rows):
         gf_ref[:, at * rows : (at + 1) * rows] = jnp.sum(recv_f[at * per : (at + 1) * per], axis=0)
 
-    blocks_wait(0, send_k).wait_send()
-    blocks_wait(1, send_g).wait_send()
+    first_wait.wait_send()
     blocks_wait(2, send_c).wait_send()
     blocks_wait(5, send_m).wait_send()
     blocks_wait(6, send_y).wait_send()
@@ -393,7 +414,7 @@
 
 def solution(mesh):
     n_ctx, n_ch = mesh.shape["ctx"], mesh.shape["ch"]
-    assert n_ctx == N_CTX
+    assert n_ctx == N_CTX and n_ch == N_CH_Y * N_CH_X
 
     def shards(query, key, value, cotangent, basis, weight, rate, skip, gain):
         rows, width = query.shape
@@ -409,7 +430,8 @@
         outside = pl.BlockSpec(memory_space=pltpu.HBM)
         wide = jax.ShapeDtypeStruct((rows, width), BF16)
         results = (wide, wide, wide, wide, jax.ShapeDtypeStruct((each, width), F32))
-        slots = [pltpu.VMEM((width, rows), F32)] * 5
+        slots = [pltpu.VMEM((n_ctx, 2 * width // n_ctx, rows), F32)]
+        slots += [pltpu.VMEM((width, rows), F32)] * 3
         last = [pltpu.VMEM((n_ctx, each, rows), F32)]
         computed = pl.pallas_call(
             functools.partial(kernel, n_ch),

time: 56 us -> 55.9 us (level)
  no operation moved by 1% of the time
where the time goes in v4:
time: 55.9 us; the launch traced here: 55.8 us
  Pallas kernels  55.1 us (99%)
  between operations  0.64 us (1%)
    pallas_call x1, Pallas kernels, shards(): pl.pallas_call(functools.partial(kernel, n_ch), out_shape=results, in_spe...  53.4 us
    pallas_call x1, Pallas kernels, shards(): pl.pallas_call(store, out_shape=results, in_specs=[inside] * 5, out_specs...  1.68 us

profile of v4, /device:TPU:1, one launch (start us, length us, event | category | flops | bytes accessed | tf_op | source)
XLA Modules:
  0.0 55.8 jit_solution(16427518983971411882)
XLA Ops:
  0.6 53.4 %shard_map.164 = (bf16[128,256]{1,0:T(8,128)(2,1)}, bf16[128,256]{1,0:T(8,128)(2,1)}, bf16[128,256]{1,0:T(8,128)(2,1)}, bf16[128,256]{1,0:T(8,128)(2,1)}, f32[2,256]{1,0:T(2,128)}) custom-call(bf16[128,256]{1,0:T(8,128)(2,1)} %q_hbm.1, bf16[128,256]{1,0:T(8,128)(2,1)} %k_hbm.1, bf16[128,256]{1,0:T(8,128)(2,1)} %v_hbm.1, bf16[128,256]{1,0:T(8,128)(2,1)} %ct_hbm.1, ...), custom_call_target="tpu_custom_call" | custom-call | tf_op jit(solution)/shard_map/pallas_call | solution.py:436
  54.1 1.7 %shard_map.165 = (bf16[128,256]{1,0:T(8,128)(2,1)}, bf16[128,256]{1,0:T(8,128)(2,1)}, bf16[128,256]{1,0:T(8,128)(2,1)}, bf16[128,256]{1,0:T(8,128)(2,1)}, f32[2,256]{1,0:T(2,128)}) custom-call(bf16[128,256]{1,0:T(8,128)(2,1)} %get-tuple-element.10.refs_0_, bf16[128,256]{1,0:T(8,128)(2,1)} %get-tuple-element.11.refs_1_, ...), custom_call_target="tpu_custom_call" | custom-call | tf_op jit(solution)/shard_map/pallas_call | solution.py:461
